TPU v7x, 256 devices: a whole 4x4x8 slice. The times are simulated.
256 devices in a mesh: ctx: 8 (over x, y_lo), exp: 32 (over z, y_hi, core).
Axes of the slice: x: 4, y: 4 (y_hi: 2, y_lo: 2; y = y_hi * 2 + y_lo), z: 8, core: 2. Of those that a mesh axis runs over, the one named last changes fastest.
Arguments:
- query: bfloat16 [4096, 12288], P('exp', 'ctx')
- latent_cache: bfloat16 [32, 4096, 576], P('exp', 'ctx')
- absorb_key: bfloat16 [64, 128, 512], P('ctx', None, 'exp'), may hold values from -0.5 to 0.5
- absorb_value: bfloat16 [64, 512, 128], P('ctx', 'exp'), may hold values from -0.25 to 0.25
- out_weight: bfloat16 [8192, 3584], P('ctx', 'exp'), may hold values from -0.0625 to 0.0625
- hidden: bfloat16 [4096, 3584], P('exp', 'ctx'), may hold values from -3 to 3
- norm_gain: float32 [3584], replicated, may hold values from 0.1 to 1.9
- block_mask: int32 [32, 32], replicated, may hold values from 0 to 1, as said below
- routes: int32 [4096, 2], P('exp'), may hold values from 0 to 127, all different within a row; in each aligned block of 128 rows (0 to 127, 128 to 255, ...) at most 3 rows name the same one
- route_weight: float32 [4096, 2], P('exp'), may hold values from 0.2 to 1
- w_gate: bfloat16 [128, 3584, 1024], P('exp', None, 'ctx'), may hold values from -0.09375 to 0.09375
- w_up: bfloat16 [128, 3584, 1024], P('exp', None, 'ctx'), may hold values from -0.09375 to 0.09375
- w_down: bfloat16 [128, 1024, 3584], P('exp', 'ctx'), may hold values from -0.1875 to 0.1875
Outputs:
- result: bfloat16 [4096, 3584], P('exp', 'ctx')
Inputs may be any that keep to these rules, and one draw needn't show every extreme that they name: block_mask[i][j] is 0 for j > i and 1 for j = i. `routes`: each row names 2 different experts; the rows of one sequence name no expert more than 3 times, a bound that some block reaches.
All inputs are finite; a program needn't handle non-finite values.
Results may differ from a plain program's by a relative error of at most 0.013.
Values may be sent and summed in bfloat16 or wider, within the bound.
A program may use at most 128 MiB of HBM per device.

v0:
```python
import math

import jax
import jax.numpy as jnp
from jax import lax
from jax.sharding import PartitionSpec as P

D = 3584
DN = 128
DR = 64
DC = 512
DV = 128
TOPK = 2
BLK = 128


def local(
    query,
    latent_cache,
    absorb_key,
    absorb_value,
    out_weight,
    hidden,
    norm_gain,
    block_mask,
    routes,
    route_weight,
    w_gate,
    w_up,
    w_down,
):
    row_count = query.shape[0]
    head_count = query.shape[1] // (DN + DR)
    share_width = hidden.shape[1]
    score_scale = 1.0 / math.sqrt(DN + DR)
    ctx_index = lax.axis_index("ctx")
    seq_length = latent_cache.shape[1] * lax.axis_size("ctx")
    absorb_key, absorb_value = (
        lax.all_gather(absorb_key, "exp", axis=2, tiled=True),
        lax.all_gather(absorb_value, "exp", axis=1, tiled=True),
    )
    queries = query.reshape(row_count, head_count, DN + DR)
    query_lat = jnp.einsum(
        "shn,hnc->shc", queries[:, :, :DN], absorb_key, preferred_element_type=jnp.float32
    ).astype(jnp.bfloat16)
    query_rope = queries[:, :, DN:]
    query_pos = seq_length - row_count + jnp.arange(row_count, dtype=jnp.int32)
    first_block = (seq_length - row_count) // BLK
    mask_blocks = block_mask[first_block : first_block + row_count // BLK]
    mask_rows = jnp.repeat(mask_blocks, BLK, axis=0)
    rows_here = lax.all_gather(latent_cache, "ctx", axis=1, tiled=True)[0]
    key_pos = jnp.arange(rows_here.shape[0], dtype=jnp.int32)
    allowed = (jnp.take(mask_rows, key_pos // BLK, axis=1) == 1) & (
        key_pos[None, :] <= query_pos[:, None]
    )
    running_max = jnp.full((row_count, head_count), -1e30, jnp.float32)
    latent = rows_here[:, :DC]
    key_rope = rows_here[:, DC:]
    scores = jnp.einsum("qhc,kc->qhk", query_lat, latent, preferred_element_type=jnp.float32)
    scores = (
        scores + jnp.einsum("qhr,kr->qhk", query_rope, key_rope, preferred_element_type=jnp.float32)
    ) * score_scale
    scores = jnp.where(allowed[:, None, :], scores, -1e30)
    new_max = jnp.maximum(running_max, jnp.max(scores, axis=-1))
    exps = jnp.where(allowed[:, None, :], jnp.exp(scores - new_max[:, :, None]), 0.0)
    new_sum = jnp.sum(exps, axis=-1)
    product = jnp.einsum(
        "qhk,kc->qhc", exps.astype(jnp.bfloat16), latent, preferred_element_type=jnp.float32
    )
    latent_out = (product / new_sum[:, :, None]).astype(jnp.bfloat16)
    attended = (
        jnp.einsum("qhc,hcv->qhv", latent_out, absorb_value, preferred_element_type=jnp.float32)
        .astype(jnp.bfloat16)
        .reshape(row_count, head_count * DV)
    )
    partial_value = jnp.dot(
        attended,
        lax.all_gather(out_weight, "exp", axis=1, tiled=True),
        preferred_element_type=jnp.float32,
    )
    placed = lax.dynamic_update_slice_in_dim(
        jnp.zeros((row_count, D), jnp.float32),
        hidden.astype(jnp.float32),
        ctx_index * share_width,
        1,
    )
    residual = lax.psum(partial_value + placed, "ctx")
    mean_square = jnp.mean(residual * residual, axis=1, keepdims=True)
    normed = (residual * lax.rsqrt(mean_square + 1e-06) * norm_gain).astype(jnp.bfloat16)
    residual_cols = lax.dynamic_slice_in_dim(residual, ctx_index * share_width, share_width, 1)
    exp_count = lax.axis_size("exp")
    local_count = w_gate.shape[0]
    expert_total = exp_count * local_count
    capacity = 3 * row_count * TOPK // (2 * expert_total)
    flat_routes = routes.reshape(-1)
    one_hot = (flat_routes[:, None] == jnp.arange(expert_total, dtype=jnp.int32)[None, :]).astype(
        jnp.int32
    )
    slot_index = jnp.sum((jnp.cumsum(one_hot, axis=0) - one_hot) * one_hot, axis=1)
    destination = flat_routes * capacity + slot_index
    token_index = jnp.arange(row_count * TOPK, dtype=jnp.int32) // TOPK
    outgoing = (
        jnp.zeros((expert_total * capacity, D), jnp.bfloat16)
        .at[destination]
        .set(normed[token_index])
    )
    outgoing = outgoing.reshape(exp_count, local_count, capacity, D)
    slots = lax.all_to_all(outgoing, "exp", split_axis=0, concat_axis=0, tiled=True)
    gate_value = jnp.einsum("sjcd,jdf->sjcf", slots, w_gate, preferred_element_type=jnp.float32)
    up_value = jnp.einsum("sjcd,jdf->sjcf", slots, w_up, preferred_element_type=jnp.float32)
    activated = (jax.nn.silu(gate_value) * up_value).astype(jnp.bfloat16)
    produced = jnp.einsum("sjcf,jfd->sjcd", activated, w_down, preferred_element_type=jnp.float32)
    returned = lax.all_to_all(produced, "exp", split_axis=0, concat_axis=0, tiled=True)
    width_back = returned.shape[3]
    row_out = returned.reshape(expert_total * capacity, width_back)[destination]
    expert_sum = jnp.sum(
        (row_out * route_weight.reshape(-1, 1)).reshape(row_count, TOPK, width_back), axis=1
    )
    expert_cols = lax.psum_scatter(expert_sum, "ctx", scatter_dimension=1, tiled=True)
    return (residual_cols + expert_cols).astype(jnp.bfloat16)


def solution(mesh):
    in_specs = (
        P("exp", "ctx"),
        P("exp", "ctx", None),
        P("ctx", None, "exp"),
        P("ctx", "exp", None),
        P("ctx", "exp"),
        P("exp", "ctx"),
        P(),
        P(),
        P("exp", None),
        P("exp", None),
        P("exp", None, "ctx"),
        P("exp", None, "ctx"),
        P("exp", "ctx", None),
    )
    out_specs = P("exp", "ctx")
    return jax.shard_map(local, mesh=mesh, in_specs=in_specs, out_specs=out_specs, check_vma=False)
```

profile of v0, /device:TPU:1, one launch (start us, length us, event | category | flops | bytes accessed | tf_op | source)
XLA Modules:
  0.0 812.4 jit_solution(2222663497705042493)
XLA Ops:
  6.5 0.7 all-gather.5.cloned.1.call-update
  7.3 0.0 all-gather.7.cloned.1.call-start
  7.3 2.1 copy.71
  9.4 0.0 all-gather.7.cloned.1.call-update
  9.5 0.0 all-gather.9.cloned.1.call-start
  9.5 0.7 all-gather.9.cloned.1.call-update
  10.2 0.0 all-gather.11.cloned.1.call-start
  10.2 0.5 all-gather.11.cloned.1.call-update
  10.8 0.0 all-reduce.2.cloned.1.call-start
  10.8 1.2 copy.69
  12.1 0.7 slice_bitcast_fusion.10
  12.8 0.1 reshape.210
  12.9 10.8 %gather_fusion = s32[4096,128]{1,0:T(8,128)S(1)} fusion(s32[128,32]{0,1:T(8,128)S(1)} %reshape.210, s32[4096]{0:T(1024)S(1)} %broadcast_clamp_fusion), kind=kCustom, calls=%fused_computation | custom fusion | bytes 4210688 | tf_op jit(solution)/shard_map/jit(_take)/gather | solution.py:53
  23.6 0.0 copy-start.2
  23.7 2.2 fusion.15
  25.8 0.9 copy.68
  26.7 0.1 copy.74
  26.9 59.4 %all-gather.5.cloned.1.call-done = bf16[8,128,512]{1,2,0:T(8,128)(2,1)} async-done(((bf16[8,128,16]{1,2,0:T(8,128)(2,1)}), bf16[8,128,512]{1,2,0:T(8,128)(2,1)}) %all-gather.5.cloned.1.call-update) | async-done | bytes 1048592 | tf_op jit(solution)/shard_map/all_gather | solution.py:39
  86.2 111.2 %all-gather.7.cloned.1.call-done = bf16[1,4096,576]{2,1,0:T(8,128)(2,1)} async-done(((bf16[1,512,576]{2,1,0:T(8,128)(2,1)}), bf16[1,4096,576]{2,1,0:T(8,128)(2,1)}) %all-gather.7.cloned.1.call-update) | async-done | bytes 4718608 | tf_op jit(solution)/shard_map/all_gather | solution.py:51
  197.4 10.3 %fusion.12 = f32[128,8,4096]{2,0,1:T(8,128)} fusion(bf16[4096,576]{1,0:T(8,128)(2,1)} %bitcast.95, bf16[8,128,512]{1,2,0:T(8,128)(2,1)} %all-gather.5.cloned.1.call-done, bf16[128,8,192]{0,2,1:T(8,128)(2,1)S(1)} %bitcast.89), kind=kOutput, calls=%fused_computation.20 | convolution fusion | flops 4429709312 | bytes 22282240 | tf_op jit(solution)/shard_map/qhc,kc->qhk/dot_general | solution.py:59
  207.7 11.7 %fusion.72 = (f32[128,8]{0,1:T(8,128)S(1)}, f32[128,8,4096]{2,0,1:T(8,128)}) fusion(f32[128,8,4096]{2,0,1:T(8,128)} %fusion.12, bf16[4096,576]{1,0:T(8,128)(2,1)} %bitcast.96, bf16[128,8,192]{0,2,1:T(8,128)(2,1)S(1)} %bitcast.90, pred[128,4096]{1,0:T(8,128)(4,1)S(1)} %copy.68), kind=kOutput, calls=%fused_computation.93 | convolution fusion | flops 553647104 | bytes 35262464 | tf_op jit(solution)/shard_map/qhr,kr->qhk/dot_general | solution.py:61
  219.3 9.2 %fusion = f32[128,8]{0,1:T(8,128)S(1)} fusion(f32[128,8,4096]{2,0,1:T(8,128)} %get-tuple-element.6, f32[128,8]{0,1:T(8,128)S(1)} %broadcast_maximum_fusion, pred[128,4096]{1,0:T(8,128)(4,1)S(1)} %copy.68), kind=kLoop, calls=%fused_computation.6 | loop fusion | flops 12581888 | bytes 17309696 | tf_op jit(solution)/shard_map/reduce_sum | solution.py:66
  228.6 45.0 %all-gather.9.cloned.1.call-done = bf16[8,512,128]{2,1,0:T(8,128)(2,1)} async-done(((bf16[8,16,128]{2,1,0:T(8,128)(2,1)}), bf16[8,512,128]{2,1,0:T(8,128)(2,1)}) %all-gather.9.cloned.1.call-update) | async-done | bytes 1048592 | tf_op jit(solution)/shard_map/all_gather | solution.py:40
  273.5 12.1 %convolution_convert_fusion.1 = bf16[8,128,128]{1,2,0:T(8,128)(2,1)S(1)} fusion(bf16[8,512,128]{2,1,0:T(8,128)(2,1)} %all-gather.9.cloned.1.call-done, f32[128,8]{0,1:T(8,128)S(1)} %fusion, f32[128,8,4096]{2,0,1:T(8,128)} %get-tuple-element.6, f32[128,8]{0,1:T(8,128)S(1)} %broadcast_maximum_fusion, pred[128,4096]{1,0:T(8,128)(4,1)S(1)} %copy.68, ...), kind=kOutput, calls=%fused_computation.35 | convolution fusion | flops 4442947584 | bytes 22814720 | tf_op jit(solution)/shard_map/qhc,hcv->qhv/dot_general | solution.py:72
  285.7 86.3 %all-gather.11.cloned.1.call-done = bf16[1024,3584]{0,1:T(8,128)(2,1)} async-done(((bf16[1024,112]{0,1:T(8,128)(2,1)}), bf16[1024,3584]{0,1:T(8,128)(2,1)}) %all-gather.11.cloned.1.call-update) | async-done | bytes 7340048 | tf_op jit(solution)/shard_map/all_gather | solution.py:78
  372.0 5.7 fusion.73
  377.6 0.0 copy-start.3
  377.6 0.1 convert_add_fusion
  377.8 0.6 add.124
  378.4 1.2 copy-done
  379.7 0.0 all-reduce.2.cloned.1.call-update
  379.7 0.1 copy.76
  379.8 0.1 eq.41
  379.9 0.1 eq.37
  380.1 0.1 copy.78
  380.2 0.2 fusion.56
  380.5 0.1 copy.75
  380.6 0.1 mul.69
  380.8 0.2 fusion.59
  381.0 92.9 %all-reduce.2.cloned.1.call-done = f32[128,3584]{1,0:T(8,128)} async-done(((f32[128,3584]{1,0:T(8,128)}), f32[128,3584]{1,0:T(8,128)}) %all-reduce.2.cloned.1.call-update) | async-done | bytes 1835024 | tf_op jit(solution)/shard_map/psum | solution.py:87
  473.9 1.7 multiply_reduce_fusion.1
  475.6 2.7 multiply_convert_fusion
  478.3 8.9 %scatter_custom_fusion = bf16[384,3584]{1,0:T(8,128)(2,1)S(1)} fusion(s32[256]{0:T(256)S(1)} %bitcast.101, bf16[128,3584]{1,0:T(8,128)(2,1)} %multiply_convert_fusion, s32[1024]{0:T(1024)S(1)} %pad_clamp_fusion.1, bf16[]{:T(256)} %constant.86.clone.1), kind=kCustom, calls=%fused_computation.28 | custom fusion | bytes 2753024 | tf_op jit(solution)/shard_map/scatter | solution.py:105
  487.2 4.1 reshape.214
  491.3 3.2 copy.80
  494.5 77.0 %all_to_all.10 = bf16[32,4,3,3584]{3,1,2,0:T(4,128)(2,1)S(1)} all-to-all(bf16[32,4,3,3584]{3,1,2,0:T(4,128)(2,1)S(1)} %copy.80), channel_id=1, replica_groups=mesh['ctx'=8,'exp'=32] {'exp'}, dimensions={0} | all-to-all | bytes 5505024 | tf_op jit(solution)/shard_map/all_to_all | solution.py:108
  571.5 1.3 fusion.21
  572.8 7.6 convolution_bitcast_fusion
  580.4 8.5 %copy.83 = f32[32,4,3,3584]{3,1,2,0:T(4,128)} copy(f32[32,4,3,3584]{3,0,2,1:T(8,128)} %convolution_bitcast_fusion) | data formatting | bytes 11010048 | tf_op jit(solution)/shard_map/sjcf,jfd->sjcd/transpose | solution.py:112
  588.9 5.7 all-to-all-start.1
  594.6 0.0 reduce-scatter.4.cloned.1.call-start
  594.7 0.1 copy.85
  594.8 124.6 %all-to-all-done.1 = f32[32,4,3,3584]{3,1,2,0:T(4,128)} async-done(((f32[32,4,3,3584]{3,1,2,0:T(4,128)}), f32[32,4,3,3584]{3,1,2,0:T(4,128)}, u32[]{:S(2)}, u32[]{:S(2)}) %all-to-all-start.1) | async-done | bytes 5505056 | tf_op jit(solution)/shard_map/all_to_all | solution.py:113
  719.4 8.4 %copy.84 = f32[32,4,3,3584]{3,2,1,0:T(4,128)} copy(f32[32,4,3,3584]{3,1,2,0:T(4,128)} %all-to-all-done.1) | data formatting | bytes 11010048 | tf_op jit(solution)/shard_map/all_to_all | solution.py:113
  727.8 9.0 %reshape.215 = f32[384,3584]{1,0:T(8,128)} reshape(f32[32,4,3,3584]{3,2,1,0:T(4,128)} %copy.84) | data formatting | bytes 11010048 | tf_op jit(solution)/shard_map/reshape | solution.py:115
  736.8 7.7 gather_fusion.1
  744.5 5.6 gather.15
  750.1 7.2 multiply_reduce_fusion
  757.3 1.7 copy.93
  759.0 0.0 reduce-scatter.4.cloned.1.call-update
  759.1 43.3 %reduce-scatter.4.cloned.1.call-done = f32[448,128]{1,0:T(8,128)} async-done(((f32[3584,128]{1,0:T(8,128)}), f32[448,128]{1,0:T(8,128)}) %reduce-scatter.4.cloned.1.call-update) | async-done | bytes 229392
  802.4 1.1 copy.94
  803.4 1.1 add_convert_fusion
  804.6 0.8 copy.86
  (27 shorter events, 0.2 us)
Async XLA Ops:
  6.5 79.7 %all-gather.5.cloned.1.call-start = ((), (), s32[]{:S(2)}) async-start(), calls=%async_computation.3 | async-start | bytes 1081344 | tf_op jit(solution)/shard_map/all_gather | solution.py:39
  7.3 190.2 %all-gather.7.cloned.1.call-start = ((), (), s32[]{:S(2)}) async-start(), calls=%async_computation.4 | async-start | bytes 5898240 | tf_op jit(solution)/shard_map/all_gather | solution.py:51
  9.5 264.1 %all-gather.9.cloned.1.call-start = ((), (), s32[]{:S(2)}) async-start(), calls=%async_computation.5 | async-start | bytes 1081344 | tf_op jit(solution)/shard_map/all_gather | solution.py:40
  10.2 361.8 %all-gather.11.cloned.1.call-start = ((), (), s32[]{:S(2)}) async-start(), calls=%async_computation.6 | async-start | bytes 7569408 | tf_op jit(solution)/shard_map/all_gather | solution.py:78
  10.8 463.1 %all-reduce.2.cloned.1.call-start = ((), (), s32[]{:S(2)}) async-start(), calls=%async_computation.7 | async-start | bytes 3670016 | tf_op jit(solution)/shard_map/psum | solution.py:87
  23.6 3.1 copy-start.2
  372.0 7.7 copy-start.4
  377.6 98.0 %copy-start.3 = (f32[3584]{0:T(1024)S(1)}, f32[3584]{0:T(1024)}, u32[]{:S(2)}) copy-start(f32[3584]{0:T(1024)} %param.19) | copy-start | bytes 43012
  378.4 1.3 copy-start
  494.5 77.1 %copy-start.1 = (bf16[4,3584,128]{2,1,0:T(8,128)(2,1)S(1)}, bf16[4,3584,128]{2,1,0:T(8,128)(2,1)}, u32[]{:S(2)}) copy-start(bf16[4,3584,128]{2,1,0:T(8,128)(2,1)} %param.23) | copy-start | bytes 11010052
  588.9 5.8 copy-start.5
  588.9 130.5 %all-to-all-start.1 = ((f32[32,4,3,3584]{3,1,2,0:T(4,128)}), f32[32,4,3,3584]{3,1,2,0:T(4,128)}, u32[]{:S(2)}, u32[]{:S(2)}) async-start(f32[32,4,3,3584]{3,1,2,0:T(4,128)} %copy.83), calls=%async_computation.1 | async-start | bytes 11010048 | tf_op jit(solution)/shard_map/all_to_all | solution.py:113
  594.6 207.8 %reduce-scatter.4.cloned.1.call-start = ((), (), s32[]{:S(2)}) async-start(), calls=%async_computation.8 | async-start | bytes 2064384
Sparse Core Ops, SparseCore 0:
  9.9 76.2 all-gather.4
  88.0 109.3 all-gather.6
  200.0 73.5 all-gather.8
  276.2 95.7 all-gather.10
  379.8 94.0 all-reduce.1
  759.2 43.1 reduce-scatter.3
where the time goes:
time: 819 us; the launch traced here: 812 us
  waiting for transfers between devices  565 us (69%)
  local copies, waits for them, and re-layouts  77.6 us (9%)
  blocking collectives  77 us (9%)
  matrix products  48.6 us (6%)
  other arithmetic  24.7 us (3%)
  between operations  14 us (2%)
    all_to_all x1, waiting for transfers between devices, local(): lax.all_to_all(produced, 'exp', split_axis=0, concat_axis=0, tiled=True)  125 us
    all_gather x1, waiting for transfers between devices, local(): rows_here = lax.all_gather(latent_cache, 'ctx', axis=1, tiled=True)[0]  111 us
    psum x1, waiting for transfers between devices, local(): residual = lax.psum(partial_value + placed, 'ctx')  92.9 us
    all_gather x1, waiting for transfers between devices, local(): lax.all_gather(out_weight, 'exp', axis=1, tiled=True)  86.3 us
    all_to_all x1, blocking collectives, local(): lax.all_to_all(outgoing, 'exp', split_axis=0, concat_axis=0, tiled=True)  77 us
    all_gather x1, waiting for transfers between devices, local(): lax.all_gather(absorb_key, 'exp', axis=2, tiled=True)  59.4 us
    unnamed x7, waiting for transfers between devices  45.3 us
    all_gather x1, waiting for transfers between devices, local(): lax.all_gather(absorb_value, 'exp', axis=1, tiled=True)  45 us
  transfers between devices with their start and end apart: 7, of which 7 were waited for; matrix products, arithmetic and copies ran while one was open for 8% of the time, Pallas kernels for 0%

commit v1 on v0

v1 whole, which is shorter than its diff:
```python
import functools
import math

import jax
import jax.numpy as jnp
import numpy as np
from jax import lax
from jax.experimental import pallas as pl
from jax.experimental.pallas import tpu as pltpu
from jax.sharding import PartitionSpec as P

D = 3584
HL = 8
DN = 128
DR = 64
DC = 512
DV = 128
TOPK = 2
BLK = 128
SHARE = 448
WIDE = 512
T = 128
NCTX = 8
NEXP = 32
CHUNK = 512
SLOTS = 384
GRID = 512
FFL = 128
MESH = pl.DeviceIdType.MESH
F32 = jnp.float32
BF16 = jnp.bfloat16
NT = (((1,), (1,)), ((), ()))
NN = (((1,), (0,)), ((), ()))
NEG = -1e30
AKV = 32
PKG = 144


def dot(a, b, dims=NN):
    return lax.dot_general(a, b, dims, preferred_element_type=F32)


def remote(src, dst, send, recv, **where):
    return pltpu.make_async_remote_copy(
        src_ref=src, dst_ref=dst, send_sem=send, recv_sem=recv, device_id=where, device_id_type=MESH
    )


def place():
    c, e = lax.axis_index("ctx"), lax.axis_index("exp")
    x, y = c // 2, c % 2
    return c, e, x, y


class Around:
    def __init__(self, x, y):
        self.x, self.y = x, y

    def at(self, dx, flip):
        yy = 1 - self.y if flip else self.y
        return ((self.x + dx + 4) % 4) * 2 + yy


class Gather:
    def __init__(self, buf, rows, send, recv, around):
        self.buf, self.rows, self.send, self.recv, self.a = buf, rows, send, recv, around
        self.me = around.at(0, False)
        self.to = {"y": around.at(0, True), "r": around.at(1, False), "l": around.at(-1, False)}

    def op(self, i):
        a, half = self.a, self.rows // 2
        table = [
            ((0, False), (0, True), "y", 0, self.rows),
            ((0, False), (-1, False), "r", 0, self.rows),
            ((0, False), (1, False), "l", 0, self.rows),
            ((0, True), (-1, True), "r", 0, self.rows),
            ((0, True), (1, True), "l", 0, self.rows),
            ((-1, False), (2, False), "r", 0, half),
            ((1, False), (2, False), "l", half, half),
            ((2, False), (2, True), "y", 0, self.rows),
        ]
        src, got, to, first, rows = table[i]
        return a.at(*src), a.at(*got), self.to[to], pl.ds(first, rows)

    def start(self, i, src=None):
        block, _, to, rows = self.op(i)
        here = self.buf.at[block, rows]
        remote(here if src is None else src, here, self.send.at[i], self.recv.at[i], ctx=to).start()

    def arrived(self, i):
        _, block, to, rows = self.op(i)
        here = self.buf.at[block, rows]
        remote(here, here, self.send.at[i], self.recv.at[i], ctx=to).wait_recv()

    def finish(self):
        for i in range(8):
            block, _, to, rows = self.op(i)
            here = self.buf.at[block, rows]
            remote(here, here, self.send.at[i], self.recv.at[i], ctx=to).wait_send()


def greet(peers):
    barrier = pltpu.get_barrier_semaphore()
    for where in peers:
        pl.semaphore_signal(barrier, inc=1, device_id=where, device_id_type=MESH)
    pl.semaphore_wait(barrier, len(peers))


def attention_kernel(
    pkg_ref,
    lat_ref,
    qn_ref,
    qr_ref,
    mask_ref,
    hid_ref,
    out_ref,
    gath,
    latb,
    qlat,
    bias,
    acc,
    mmax,
    lsum,
    attn,
    parts,
    got,
    own_sem,
    w_send,
    w_recv,
    l_send,
    l_recv,
    r_send,
    r_recv,
    *,
    scale,
):
    c, e, x, y = place()
    z, h, k = e // 4, (e // 2) % 2, e % 2
    around = Around(x, y)

    def eid(zz, hh, kk):
        return ((zz + 16) % 8) * 4 + hh * 2 + kk

    up, down = eid(z + 1, h, k), eid(z - 1, h, k)
    partner, sibling = eid(z, 1 - h, k), eid(z, h, 1 - k)
    greet(
        [{"exp": d} for d in (up, down, partner, sibling)]
        + [{"ctx": (c + i) % NCTX} for i in range(1, NCTX)]
    )

    rows_of = (pl.ds(0, AKV), pl.ds(AKV, PKG - AKV))

    def slot(off, flip, other=False):
        return eid(z + off, 1 - h if flip else h, 1 - k if other else k)

    def wcopy(p, ident, block, to, src=None):
        here = gath.at[block, rows_of[p]]
        return remote(
            here if src is None else src.at[rows_of[p]],
            here,
            w_send.at[p, ident],
            w_recv.at[p, ident],
            exp=to,
        )

    def ring_id(sign, off, flip):
        if off == 4:
            return 7 if sign > 0 else 14
        return (1 if sign > 0 else 8) + (off - 1) * 2 + int(flip)

    def sib_id(off, flip):
        return 16 + (off % 8) * 2 + int(flip)

    started = []

    def send_on(p, off, flip, sign, nxt, src=None):
        block, to = slot(-sign * off, flip), (up if sign > 0 else down)
        ident = ring_id(sign, nxt, flip)
        wcopy(p, ident, block, to, src).start()
        started.append((p, ident, block, to))

    def send_sibling(p, off, flip, src=None):
        block = slot(off, flip)
        wcopy(p, sib_id(off, flip), block, sibling, src).start()
        started.append((p, sib_id(off, flip), block, sibling))

    def weights_first(p):
        wcopy(p, 0, e, partner, pkg_ref).start()
        started.append((p, 0, e, partner))
        for sign in (1, -1):
            send_on(p, 0, False, sign, 1, pkg_ref)
        send_sibling(p, 0, False, pkg_ref)

    def weights_partner(p):
        wcopy(p, 0, slot(0, True), partner).wait_recv()
        for sign in (1, -1):
            send_on(p, 0, True, sign, 1)
        send_sibling(p, 0, True)

    def weights_ring(p, off, flip):
        for sign in (1, -1):
            if off == 4 and flip != (sign < 0):
                continue
            wcopy(p, ring_id(sign, off, flip), slot(-sign * off, flip), partner).wait_recv()
            if off < 3 or (off == 3 and flip == (sign < 0)):
                send_on(p, off, flip, sign, off + 1)
            send_sibling(p, -sign * off, flip)

    def weights_sibling(p, off):
        for flip in (False, True):
            wcopy(p, sib_id(off, flip), slot(off, flip, True), sibling).wait_recv()

    lat = Gather(latb, DC + DR, l_send, l_recv, around)

    own_pkg = pltpu.make_async_copy(pkg_ref, gath.at[e], own_sem.at[0])
    own_lat = pltpu.make_async_copy(lat_ref, latb.at[c], own_sem.at[1])
    own_pkg.start()
    own_lat.start()
    weights_first(0)
    for i in range(3):
        lat.start(i, lat_ref)
    weights_first(1)

    token = lax.broadcasted_iota(jnp.int32, (T, CHUNK), 0)
    position = lax.broadcasted_iota(jnp.int32, (T, CHUNK), 1)

    def fill(i, carry):
        open_row = mask_ref[pl.ds(i, 1), :] > 0.0
        seen = (position + i * CHUNK) <= (token + (NCTX * CHUNK - T))
        bias[i] = jnp.where(open_row & seen, 1.0, 0.0)
        return carry

    lax.fori_loop(0, NCTX, fill, 0)

    weights_partner(0)
    weights_ring(0, 1, False)
    weights_ring(0, 1, True)
    lat.arrived(0)
    lat.start(3)
    lat.start(4)
    weights_ring(0, 2, False)
    weights_ring(0, 2, True)
    weights_partner(1)
    weights_ring(0, 3, False)
    weights_ring(0, 3, True)
    lat.arrived(1)
    lat.start(5)
    lat.arrived(2)
    lat.start(6)
    weights_ring(0, 4, False)
    weights_ring(0, 4, True)
    own_pkg.wait()
    own_lat.wait()
    for off in range(8):
        weights_sibling(0, off)

    def absorb(head, carry):
        cols = pl.ds(pl.multiple_of(head * DN, DN), DN)
        rows = pl.ds(pl.multiple_of(head * T, T), T)
        weight = gath[:, 0:16, cols].reshape(DC, DN)
        qlat[rows, :] = dot(qn_ref[rows, :], weight, NT).astype(BF16)
        return carry

    lax.fori_loop(0, HL, absorb, 0)

    factor = scale * math.log2(math.e)

    def attend(first, blocks, lo, hi):
        def body(i, carry):
            rows = pl.ds(pl.multiple_of(i * 2 * T, 2 * T), 2 * T)
            ql, qr = qlat[rows, :], qr_ref[rows, :]
            scores = []
            for b in blocks:
                s = dot(ql, latb[b, 0:DC, :], NT) + dot(qr, latb[b, DC : DC + DR, :])
                allowed = bias[b] > 0.0
                allowed = jnp.concatenate([allowed, allowed], axis=0)
                scores.append(jnp.where(allowed, s * factor, NEG))
            top = jnp.max(jnp.maximum(*scores), axis=1, keepdims=True)
            if not first:
                old = mmax[rows, 0:1]
                top = jnp.maximum(old, top)
            probs = [jnp.exp2(s - top) for s in scores]
            total = jnp.sum(probs[0] + probs[1], axis=1, keepdims=True)
            product = sum(
                dot(p.astype(BF16), latb[b, 0:DC, :]) for p, b in zip(probs, blocks, strict=True)
            )
            if not first:
                shrink = jnp.exp2(old - top)
                total = total + lsum[rows, 0:1] * shrink
                product = product + acc[rows, :] * shrink
            mmax[rows, :] = jnp.broadcast_to(top, (2 * T, 128))
            lsum[rows, :] = jnp.broadcast_to(total, (2 * T, 128))
            acc[rows, :] = product
            return carry

        lax.fori_loop(lo, hi, body, 0)

    def pair(dx):
        return [around.at(dx, False), around.at(dx, True)]

    attend(True, pair(0), 0, 4)
    weights_ring(1, 1, False)
    lat.arrived(4)
    attend(False, pair(1), 0, 4)
    weights_ring(1, 1, True)
    lat.arrived(5)
    lat.arrived(6)
    lat.start(7)
    lat.arrived(3)
    attend(False, pair(-1), 0, 4)
    weights_ring(1, 2, False)
    lat.arrived(7)
    attend(False, pair(2), 0, 4)
    weights_ring(1, 2, True)
    lat.finish()

    def values(head, carry):
        cols = pl.ds(pl.multiple_of(head * DV, DV), DV)
        rows = pl.ds(pl.multiple_of(head * T, T), T)
        weight = gath[:, 16:32, cols].reshape(DC, DV)
        latent_out = (acc[rows, :] / lsum[rows, 0:1]).astype(BF16)
        attn[:, cols] = dot(latent_out, weight).astype(BF16)
        return carry

    lax.fori_loop(0, HL, values, 0)

    def rcopy(dest, source):
        return remote(parts.at[dest], got.at[source], r_send.at[dest], r_recv.at[source], ctx=dest)

    def project(off):
        weights_sibling(1, off)
        dest = (z + off + 8) % 8
        weight = gath[pl.ds(dest * 4, 4), AKV:PKG, :].reshape(SHARE, HL * DV)
        partial = dot(attn[...], weight, NT)
        parts[dest, :, 0:SHARE] = partial.astype(BF16)
        parts[dest, :, SHARE:WIDE] = jnp.zeros((T, WIDE - SHARE), BF16)

        @pl.when(dest != c)
        def _():
            rcopy(dest, c).start()

        @pl.when(dest == c)
        def _():
            got[c] = parts[dest]

    project(0)
    weights_ring(1, 3, False)
    project(1)
    project(-1)
    weights_ring(1, 3, True)
    project(2)
    project(-2)
    weights_ring(1, 4, False)
    weights_ring(1, 4, True)
    project(3)
    project(-3)
    project(4)

    for i in range(1, NCTX):
        source = (c + i) % NCTX
        remote(
            got.at[source], got.at[source], r_send.at[source], r_recv.at[source], ctx=source
        ).wait_recv()
    total = hid_ref[...].astype(F32)
    for i in range(NCTX):
        total = total + got[i, :, 0:SHARE].astype(F32)
    out_ref[...] = total

    for p, ident, block, to in started:
        wcopy(p, ident, block, to).wait_send()
    for i in range(1, NCTX):
        dest = (c + i) % NCTX
        rcopy(dest, c).wait_send()


def expert_kernel(
    r_ref,
    gain_ref,
    place_row_ref,
    place_col_ref,
    weight_ref,
    perm_ref,
    unperm_ref,
    wg_hbm,
    wu_hbm,
    wd_hbm,
    out_ref,
    wg,
    wu,
    wd,
    xs,
    rx,
    xa,
    gate,
    up,
    tails,
    act,
    pd,
    t0,
    t1,
    t2,
    t3,
    t4,
    t5,
    t6,
    t7,
    ys,
    back,
    own_sem,
    a_send,
    a_recv,
    g_send,
    g_recv,
    s_send,
    s_recv,
    b_send,
    b_recv,
):
    c, e, x, y = place()
    around = Around(x, y)
    weights = [
        pltpu.make_async_copy(src, dst, own_sem.at[i])
        for i, (src, dst) in enumerate(((wg_hbm, wg), (wu_hbm, wu), (wd_hbm, wd)))
    ]
    for w in weights:
        w.start()

    barrier = pltpu.get_barrier_semaphore()

    def hello(i, carry):
        pl.semaphore_signal(
            barrier, inc=1, device_id={"exp": (e + i) % NEXP}, device_id_type=MESH
        )
        return carry

    lax.fori_loop(1, NEXP, hello, 0)
    for i in range(1, NCTX):
        pl.semaphore_signal(
            barrier, inc=1, device_id={"ctx": (c + i) % NCTX}, device_id_type=MESH
        )

    resid = r_ref[...]
    squares = jnp.sum(resid * resid, axis=1, keepdims=True)
    high = squares.astype(BF16).astype(F32)
    low = squares - high
    lane = lax.broadcasted_iota(jnp.int32, (T, WIDE - SHARE), 1)
    tail = jnp.where(lane == 0, high, jnp.where(lane == 1, low, 0.0))
    scaled = jnp.concatenate([resid * gain_ref[...], tail], axis=1).astype(BF16)
    where = lax.broadcasted_iota(jnp.int32, (GRID, T), 0)
    chosen = (where == place_row_ref[0:1, :]) | (where == place_row_ref[1:2, :])
    xs[...] = dot(jnp.where(chosen, 1.0, 0.0).astype(BF16), scaled).astype(BF16)

    pl.semaphore_wait(barrier, NEXP - 1 + NCTX - 1)

    def rows16(i):
        return pl.ds(pl.multiple_of(i * 16, 16), 16)

    def exchange(src, dst, send, recv):
        def make(i):
            to = (e + i) % NEXP
            return remote(src.at[rows16(to)], dst.at[rows16(e)], send.at[i], recv.at[i], exp=to)

        def go(i, carry):
            make(i).start()
            return carry

        def land(i, carry):
            frm = (e + NEXP - i) % NEXP
            remote(
                dst.at[rows16(frm)], dst.at[rows16(frm)], send.at[i], recv.at[i], exp=frm
            ).wait_recv()
            return carry

        def left(i, carry):
            make(i).wait_send()
            return carry

        lax.fori_loop(1, NEXP, go, 0)
        dst[rows16(e), :] = src[rows16(e), :]
        lax.fori_loop(1, NEXP, land, 0)
        return lambda: lax.fori_loop(1, NEXP, left, 0)

    a_left = exchange(xs, rx, a_send, a_recv)
    xa[c] = dot(perm_ref[...], rx[...]).astype(BF16)

    ga = Gather(xa, SLOTS, g_send, g_recv, around)
    for i in range(3):
        ga.start(i)

    def feed(block, first=False):
        rows_c = pl.ds(pl.multiple_of(block * SHARE, SHARE), SHARE)

        def body(j, carry):
            rows = pl.ds(pl.multiple_of(j * 96, 96), 96)
            lhs = xa[block, rows, 0:SHARE]
            g = dot(lhs, wg[j, rows_c, :])
            u = dot(lhs, wu[j, rows_c, :])
            t = xa[block, rows, 384:WIDE].astype(F32)
            if first:
                gate[rows, :], up[rows, :], tails[rows, :] = g, u, t
            else:
                gate[rows, :] += g
                up[rows, :] += u
                tails[rows, :] += t
            return carry

        lax.fori_loop(0, 4, body, 0)

    for w in weights:
        w.wait()
    feed(c, True)
    ga.arrived(0)
    ga.start(3)
    ga.start(4)
    feed(around.at(0, True))
    ga.arrived(1)
    ga.start(5)
    ga.arrived(2)
    ga.start(6)
    feed(around.at(-1, False))
    feed(around.at(1, False))
    ga.arrived(5)
    ga.arrived(6)
    ga.start(7)
    feed(around.at(2, False))
    ga.arrived(3)
    feed(around.at(-1, True))
    ga.arrived(4)
    feed(around.at(1, True))
    ga.arrived(7)
    feed(around.at(2, True))
    ga.finish()
    a_left()

    lanes = lax.broadcasted_iota(jnp.int32, (SLOTS, 128), 1)
    kept = jnp.where((lanes == 64) | (lanes == 65), tails[...], 0.0)
    inv = lax.rsqrt(jnp.sum(kept, axis=1, keepdims=True) / D + 1e-06)
    gv = gate[...] * inv
    act[...] = (gv / (1.0 + jnp.exp(-gv)) * (up[...] * inv)).astype(BF16)

    def produce(xx):
        cols = pl.ds(pl.multiple_of(xx * 2 * SHARE, 2 * SHARE), 2 * SHARE)

        def body(j, carry):
            rows = pl.ds(pl.multiple_of(j * 96, 96), 96)
            both = dot(act[rows, :], wd[j, :, cols]).astype(BF16)
            pd[xx * 2, rows, 0:SHARE] = both[:, 0:SHARE]
            pd[xx * 2 + 1, rows, 0:SHARE] = both[:, SHARE:]
            pd[xx * 2, rows, SHARE:WIDE] = jnp.zeros((96, WIDE - SHARE), BF16)
            pd[xx * 2 + 1, rows, SHARE:WIDE] = jnp.zeros((96, WIDE - SHARE), BF16)
            return carry

        lax.fori_loop(0, 4, body, 0)

    half = SLOTS // 2
    lo, hi, whole = pl.ds(0, half), pl.ds(half, half), pl.ds(0, SLOTS)
    yp, xr, xl = around.at(0, True), around.at(1, False), around.at(-1, False)
    sends = [
        (around.at(2, True), whole, t0, yp),
        (around.at(1, True), whole, t1, xr),
        (around.at(-1, True), whole, t2, xl),
        (around.at(2, False), lo, t3, xr),
        (around.at(2, False), hi, t4, xl),
        (around.at(0, True), whole, t5, yp),
        (around.at(1, False), hi, t6.at[hi], xr),
        (around.at(-1, False), lo, t7.at[lo], xl),
        (around.at(1, False), lo, t6.at[lo], xr),
        (around.at(-1, False), hi, t7.at[hi], xl),
    ]

    def scopy(i):
        block, rows, dst, to = sends[i]
        return remote(pd.at[block, rows], dst, s_send.at[i], s_recv.at[i], ctx=to)

    def sgot(i):
        _, _, dst, to = sends[i]
        remote(dst, dst, s_send.at[i], s_recv.at[i], ctx=to).wait_recv()

    def add(block, rows, *terms):
        total = pd[block, rows, :].astype(F32)
        for t in terms:
            total = total + t[...].astype(F32)
        pd[block, rows, :] = total.astype(BF16)

    produce((x + 2) % 4)
    scopy(0).start()
    produce((x + 1) % 4)
    scopy(1).start()
    scopy(6).start()
    produce((x + 3) % 4)
    scopy(2).start()
    scopy(7).start()
    sgot(0)
    add(around.at(2, False), whole, t0)
    scopy(3).start()
    scopy(4).start()
    produce(x)
    sgot(1)
    sgot(2)
    add(around.at(0, True), whole, t1, t2)
    scopy(5).start()
    sgot(3)
    add(around.at(1, False), lo, t3)
    scopy(8).start()
    sgot(4)
    add(around.at(-1, False), hi, t4)
    scopy(9).start()
    for i in (5, 6, 7, 8, 9):
        sgot(i)
    total = pd[c].astype(F32)
    for t in (t5, t6, t7):
        total = total + t[...].astype(F32)
    ys[...] = dot(unperm_ref[...], total.astype(BF16)).astype(BF16)

    b_left = exchange(ys, back, b_send, b_recv)
    spots = lax.broadcasted_iota(jnp.int32, (T, GRID), 1)
    result = resid
    for kk in range(TOPK):
        picked = jnp.where(spots == place_col_ref[:, kk : kk + 1], 1.0, 0.0).astype(BF16)
        result = result + dot(picked, back[...])[:, 0:SHARE] * weight_ref[:, kk : kk + 1]
    out_ref[...] = result.astype(BF16)

    for i in range(10):
        scopy(i).wait_send()
    b_left()


def permutations():
    perm = np.zeros((SLOTS, GRID), np.float32)
    for j in range(4):
        for s in range(NEXP):
            for i in range(3):
                perm[j * 96 + s * 3 + i, s * 16 + j * 4 + i] = 1.0
    return perm


VMEM = pl.BlockSpec(memory_space=pltpu.VMEM)
ANY = pl.BlockSpec(memory_space=pl.ANY)


def local(
    query,
    latent_cache,
    absorb_key,
    absorb_value,
    out_weight,
    hidden,
    norm_gain,
    block_mask,
    routes,
    route_weight,
    w_gate,
    w_up,
    w_down,
):
    ctx_index = lax.axis_index("ctx")
    scale = 1.0 / math.sqrt(DN + DR)
    pkg = jnp.concatenate(
        [
            absorb_key.transpose(2, 0, 1).reshape(16, HL * DN),
            absorb_value.transpose(1, 0, 2).reshape(16, HL * DV),
            out_weight.T,
        ],
        axis=0,
    )
    latent = jnp.concatenate([latent_cache[0, :, :DC], latent_cache[0, :, DC:].T], axis=0)
    queries = query.reshape(T, HL, DN + DR).transpose(1, 0, 2).reshape(HL * T, DN + DR)
    mask = jnp.repeat(block_mask[-1].astype(F32), BLK).reshape(NCTX, CHUNK)

    flat = routes.reshape(-1)
    one_hot = (flat[:, None] == jnp.arange(128, dtype=jnp.int32)[None, :]).astype(BF16)
    before = jnp.tril(jnp.ones((T * TOPK, T * TOPK), BF16), -1)
    count = jnp.dot(before, one_hot, preferred_element_type=F32)
    slot = jnp.sum(count * one_hot.astype(F32), axis=1).astype(jnp.int32)
    places = (flat * 4 + slot).reshape(T, TOPK)
    place_row = jnp.concatenate([places.T, jnp.full((6, T), -1, jnp.int32)], axis=0)
    gain = lax.dynamic_slice_in_dim(norm_gain, ctx_index * SHARE, SHARE, 0)[None, :]

    residual = pl.pallas_call(
        functools.partial(attention_kernel, scale=scale),
        out_shape=jax.ShapeDtypeStruct((T, SHARE), F32),
        in_specs=[ANY, ANY, VMEM, VMEM, VMEM, VMEM],
        out_specs=VMEM,
        scratch_shapes=[
            pltpu.VMEM((NEXP, PKG, HL * DV), BF16),
            pltpu.VMEM((NCTX, DC + DR, CHUNK), BF16),
            pltpu.VMEM((HL * T, DC), BF16),
            pltpu.VMEM((NCTX, T, CHUNK), F32),
            pltpu.VMEM((HL * T, DC), F32),
            pltpu.VMEM((HL * T, 128), F32),
            pltpu.VMEM((HL * T, 128), F32),
            pltpu.VMEM((T, HL * DV), BF16),
            pltpu.VMEM((NCTX, T, WIDE), BF16),
            pltpu.VMEM((NCTX, T, WIDE), BF16),
            pltpu.SemaphoreType.DMA((2,)),
            pltpu.SemaphoreType.DMA((2, 32)),
            pltpu.SemaphoreType.DMA((2, 32)),
            pltpu.SemaphoreType.DMA((8,)),
            pltpu.SemaphoreType.DMA((8,)),
            pltpu.SemaphoreType.DMA((8,)),
            pltpu.SemaphoreType.DMA((8,)),
        ],
        compiler_params=pltpu.CompilerParams(
            collective_id=0, has_side_effects=True, vmem_limit_bytes=48 * 1024 * 1024
        ),
        name="attention",
    )(pkg, latent, queries[:, :DN], queries[:, DN:], mask, hidden)

    perm = permutations()
    dma = pltpu.SemaphoreType.DMA
    return pl.pallas_call(
        expert_kernel,
        out_shape=jax.ShapeDtypeStruct((T, SHARE), BF16),
        in_specs=[VMEM] * 7 + [ANY] * 3,
        out_specs=VMEM,
        scratch_shapes=[
            pltpu.VMEM((4, D, FFL), BF16),
            pltpu.VMEM((4, D, FFL), BF16),
            pltpu.VMEM((4, FFL, D), BF16),
            pltpu.VMEM((GRID, WIDE), BF16),
            pltpu.VMEM((GRID, WIDE), BF16),
            pltpu.VMEM((NCTX, SLOTS, WIDE), BF16),
            pltpu.VMEM((SLOTS, FFL), F32),
            pltpu.VMEM((SLOTS, FFL), F32),
            pltpu.VMEM((SLOTS, 128), F32),
            pltpu.VMEM((SLOTS, FFL), BF16),
            pltpu.VMEM((NCTX, SLOTS, WIDE), BF16),
            pltpu.VMEM((SLOTS, WIDE), BF16),
            pltpu.VMEM((SLOTS, WIDE), BF16),
            pltpu.VMEM((SLOTS, WIDE), BF16),
            pltpu.VMEM((SLOTS // 2, WIDE), BF16),
            pltpu.VMEM((SLOTS // 2, WIDE), BF16),
            pltpu.VMEM((SLOTS, WIDE), BF16),
            pltpu.VMEM((SLOTS, WIDE), BF16),
            pltpu.VMEM((SLOTS, WIDE), BF16),
            pltpu.VMEM((GRID, WIDE), BF16),
            pltpu.VMEM((GRID, WIDE), BF16),
            dma((3,)),
            dma((32,)),
            dma((32,)),
            dma((8,)),
            dma((8,)),
            dma((10,)),
            dma((10,)),
            dma((32,)),
            dma((32,)),
        ],
        compiler_params=pltpu.CompilerParams(
            collective_id=1, has_side_effects=True, vmem_limit_bytes=48 * 1024 * 1024
        ),
        name="experts",
    )(
        residual,
        gain,
        place_row,
        places,
        route_weight,
        jnp.asarray(perm, BF16),
        jnp.asarray(perm.T, BF16),
        w_gate,
        w_up,
        w_down,
    )


def solution(mesh):
    in_specs = (
        P("exp", "ctx"),
        P("exp", "ctx", None),
        P("ctx", None, "exp"),
        P("ctx", "exp", None),
        P("ctx", "exp"),
        P("exp", "ctx"),
        P(),
        P(),
        P("exp", None),
        P("exp", None),
        P("exp", None, "ctx"),
        P("exp", None, "ctx"),
        P("exp", "ctx", None),
    )
    out_specs = P("exp", "ctx")
    return jax.shard_map(local, mesh=mesh, in_specs=in_specs, out_specs=out_specs, check_vma=False)
```

time: 819 us -> 207 us (0.25)
  waiting for transfers between devices: 565 us -> 0 us
  Pallas kernels: 0 us -> 196 us
  blocking collectives: 77 us -> 0 us
  local copies, waits for them, and re-layouts: 77.6 us -> 8.77 us
  matrix products: 48.6 us -> 0.3 us
  other arithmetic: 24.7 us -> 1.73 us
  between operations: 14 us -> 0.19 us
    all_gather x4 -> x0, waiting for transfers between devices: 302 us -> none  [the longest x1 111 us: local(): rows_here = lax.all_gather(latent_cache, 'ctx', axis=1, tiled=True)[0]]
    pallas_call x0 -> x2, Pallas kernels: none -> 196 us  [the longest x1 103 us: local(): pl.pallas_call(expert_kernel, out_shape=jax.ShapeDtypeStruct((T, SHARE),...]
    all_to_all x1 -> x0, waiting for transfers between devices: 125 us -> none  [local(): lax.all_to_all(produced, 'exp', split_axis=0, concat_axis=0, tiled=True)]
    psum x1 -> x0, waiting for transfers between devices: 92.9 us -> none  [local(): residual = lax.psum(partial_value + placed, 'ctx')]
    all_to_all x1 -> x0, blocking collectives: 77 us -> none  [local(): lax.all_to_all(outgoing, 'exp', split_axis=0, concat_axis=0, tiled=True)]
    dot_general x6 -> x1, matrix products: 48.6 us -> 0.3 us  [local(): count = jnp.dot(before, one_hot, preferred_element_type=F32)]
    unnamed x7 -> x0, waiting for transfers between devices: 45.3 us -> none
    gather x3 -> x0, local copies, waits for them, and re-layouts: 24 us -> none  [the longest x2 13.3 us: local(): row_out = returned.reshape(expert_total * capacity, width_back)[destination]]
  transfers between devices with their start and end apart: 7 -> 0, of which waited for: 7 -> 0; matrix products, arithmetic and copies ran while one was open for 8% -> 0% of each run, Pallas kernels for 0% -> 0%
where the time goes in v1:
time: 207 us
  Pallas kernels  196 us (95%)
  local copies, waits for them, and re-layouts  8.77 us (4%)
    pallas_call x1, Pallas kernels, local(): pl.pallas_call(expert_kernel, out_shape=jax.ShapeDtypeStruct((T, SHARE),...  103 us
    pallas_call x1, Pallas kernels, local(): pl.pallas_call(functools.partial(attention_kernel, scale=scale), out_shap...  92.5 us

profile of v1, /device:TPU:1, one launch (start us, length us, event | category | flops | bytes accessed | tf_op | source)
XLA Modules:
  0.0 206.8 jit_solution(6145939371938421922)
XLA Ops:
  0.0 0.0 copy-start
  0.0 0.0 copy-start.4
  0.0 0.0 copy-start.5
  0.0 0.7 copy-done
  0.8 0.8 copy_bitcast_fusion
  1.5 1.0 pad_maximum_fusion.1.pkg_ref
  2.5 0.8 slice_bitcast_fusion
  3.3 1.1 slice.15
  4.4 0.0 copy-start.6
  4.4 0.2 copy.52
  4.6 0.0 copy-start.7
  4.7 0.0 copy-start.2
  4.7 0.0 copy-start.3
  4.7 0.0 copy-done.4
  4.7 0.2 copy.43
  5.0 0.2 copy.44
  5.2 0.7 convert_reduce_fusion
  5.9 0.1 convert_element_type.21
  6.0 0.1 copy.45
  6.1 0.1 broadcast_bitcast_fusion.mask_ref
  6.2 0.0 copy-done.5
  6.2 0.1 copy.46.hid_ref
  6.3 92.5 %attention.1.r_ref = f32[128,448]{1,0:T(8,128)S(1)} custom-call(bf16[144,1024]{1,0:T(8,128)(2,1)S(1)} %pad_maximum_fusion.1.pkg_ref, bf16[576,512]{1,0:T(8,128)(2,1)S(1)} %pad_maximum_fusion.lat_ref, bf16[1024,128]{1,0:T(8,128)(2,1)S(1)} %slice.20.qn_ref, bf16[1024,64]{1,0:T(8,128)(2,1)S(1)} %slice.21.qr_ref, f32[8,512]{1,0:T(8,128)S(1)} %broadcast_bitcast_fusion.mask_ref, ...), custom_call_target="tpu_custom_call" | custom-call | tf_op jit(solution)/shard_map/attention/pallas_call | solution.py:679
  98.8 0.8 dynamic_slice.3
  99.6 0.0 copy-done.6
  99.6 0.1 copy.48
  99.7 0.1 copy.47
  99.9 0.1 eq.15
  100.0 0.3 fusion
  100.3 0.1 convert_element_type.25
  100.5 0.1 copy.53
  100.5 0.0 copy-done.7
  100.6 0.1 copy.50.weight_ref
  100.7 0.0 copy-done.2
  100.7 0.0 copy-done.3
  100.7 0.0 copy-start.1
  100.7 2.0 copy-done.1
  102.7 103.3 %experts.1 = bf16[128,448]{1,0:T(8,128)(2,1)S(1)} custom-call(f32[128,448]{1,0:T(8,128)S(1)} %attention.1.r_ref, f32[1,448]{1,0:T(1,128)S(1)} %bitcast.27, s32[8,128]{1,0:T(8,128)S(1)} %concatenate.11.clone.place_row_ref, s32[128,2]{1,0:T(8,128)S(1)} %add.21.place_col_ref, f32[128,2]{1,0:T(8,128)S(1)} %copy.50.weight_ref, bf16[384,512]{1,0:T(8,128)(2,1)S(1)} %copy-done.2, ...), custom_call_target="tpu_custom_call" | custom-call | tf_op jit(solution)/shard_map/experts/pallas_call | solution.py:711
  206.0 0.8 copy.51
  (8 shorter events, 0.1 us)
Async XLA Ops:
  0.0 0.8 copy-start
  0.0 4.7 %copy-start.4 = (bf16[128,1536]{1,0:T(8,128)(2,1)S(1)}, bf16[128,1536]{1,0:T(8,128)(2,1)}, u32[]{:S(2)}) copy-start(bf16[128,1536]{1,0:T(8,128)(2,1)} %param.15) | copy-start | bytes 1179652
  0.0 6.2 %copy-start.5 = (bf16[128,448]{0,1:T(8,128)(2,1)S(1)}, bf16[128,448]{0,1:T(8,128)(2,1)}, u32[]{:S(2)}) copy-start(bf16[128,448]{0,1:T(8,128)(2,1)} %param.20) | copy-start | bytes 344068
  4.4 95.2 %copy-start.6 = (s32[128,2]{0,1:T(2,128)S(1)}, s32[128,2]{0,1:T(2,128)}, u32[]{:S(2)}) copy-start(s32[128,2]{0,1:T(2,128)} %param.23) | copy-start | bytes 3076
  4.6 95.9 %copy-start.7 = (f32[128,2]{0,1:T(2,128)S(1)}, f32[128,2]{0,1:T(2,128)}, u32[]{:S(2)}) copy-start(f32[128,2]{0,1:T(2,128)} %param.24) | copy-start | bytes 3076
  4.7 96.0 %copy-start.2 = (bf16[384,512]{1,0:T(8,128)(2,1)S(1)}, bf16[384,512]{1,0:T(8,128)(2,1)}, u32[]{:S(2)}) copy-start(bf16[384,512]{1,0:T(8,128)(2,1)} %constant.29.clone.perm_ref) | copy-start | bytes 1179652
  4.7 96.0 %copy-start.3 = (bf16[512,384]{1,0:T(8,128)(2,1)S(1)}, bf16[512,384]{1,0:T(8,128)(2,1)}, u32[]{:S(2)}) copy-start(bf16[512,384]{1,0:T(8,128)(2,1)} %constant.30.clone.unperm_ref) | copy-start | bytes 1179652
  100.7 2.0 copy-start.1

commit v2 on v0

v2 whole, which is shorter than its diff:
```python
import functools
import math

import jax
import jax.numpy as jnp
import numpy as np
from jax import lax
from jax.experimental import pallas as pl
from jax.experimental.pallas import tpu as pltpu
from jax.sharding import PartitionSpec as P

D = 3584
HL = 8
DN = 128
DR = 64
DC = 512
DV = 128
TOPK = 2
BLK = 128
SHARE = 448
WIDE = 512
T = 128
NCTX = 8
NEXP = 32
CHUNK = 512
SLOTS = 384
GRID = 512
FFL = 128
MESH = pl.DeviceIdType.MESH
F32 = jnp.float32
BF16 = jnp.bfloat16
NT = (((1,), (1,)), ((), ()))
NN = (((1,), (0,)), ((), ()))
NEG = -1e38
WO = 112
ROWS = 96
MASKED = DC + DR
CAUSAL = MASKED + 16
DEPTH = CAUSAL + T
HALF_LAT = (DC + DR) // 2
PIECE_ROWS = {1: (0, 32), 2: (32, 32), 4: (64, 48), 5: (0, WO)}
LAST_PIECE = 4

PLAN = (
    ("first", 0), ("latents", 0), ("latents", 1), ("first", 1), ("first", 2), ("prepare",), ("ring", 0, 1, 0),
    ("partner", 0), ("first", 4), ("ring", 0, 2, 0), ("ring", 0, 1, 1), ("ring", 1, 1, 0), ("first", 3),
    ("halves", 0), ("spread", 0), ("ring", 0, 3, 0), ("ring", 0, 2, 1), ("ring", 2, 1, 0), ("ring", 1, 2, 0),
    ("ring", 0, 3, 1), ("ring", 3, 1, 0), ("ring", 4, 1, 0), ("halves", 1), ("ring", 2, 2, 0), ("spread", 1),
    ("ring", 1, 3, 0), ("partner", 1), ("far", 0), ("cross", 0), ("partner", 2), ("absorb",), ("partner", 3),
    ("partner", 4), ("attend", 0, 0), ("ring", 3, 2, 0), ("attend", 0, 1), ("ring", 1, 1, 1),
    ("ring", 4, 2, 0), ("attend", 0, 2), ("attend", 0, 3), ("cross", 1), ("ring", 2, 1, 1), ("attend", 1, 0),
    ("ring", 3, 1, 1), ("ring", 4, 1, 1), ("attend", 1, 1), ("ring", 1, 2, 1), ("attend", 1, 2),
    ("ring", 2, 3, 0), ("attend", 1, 3), ("ring", 2, 2, 1), ("attend", 2, 0), ("ring", 3, 2, 1),
    ("ring", 3, 3, 0), ("attend", 2, 1), ("ring", 4, 2, 1), ("attend", 2, 2), ("ring", 4, 3, 0),
    ("attend", 2, 3), ("attend", 3, 0), ("ring", 1, 3, 1), ("ring", 2, 3, 1), ("ring", 3, 3, 1),
    ("attend", 3, 1), ("attend", 3, 2), ("ring", 4, 3, 1), ("attend", 3, 3), ("far", 1), ("far", 2),
    ("far", 3), ("far", 4), ("values",), ("project", 0), ("project", 1), ("project", -1), ("project", 2),
    ("project", -2), ("project", 3), ("project", -3), ("project", 4),
)


def dot(a, b, dims=NN):
    return lax.dot_general(a, b, dims, preferred_element_type=F32)


def remote(src, dst, send, recv, **where):
    return pltpu.make_async_remote_copy(
        src_ref=src, dst_ref=dst, send_sem=send, recv_sem=recv, device_id=where, device_id_type=MESH
    )


def place():
    c, e = lax.axis_index("ctx"), lax.axis_index("exp")
    x, y = c // 2, c % 2
    return c, e, x, y


class Around:
    def __init__(self, x, y):
        self.x, self.y = x, y

    def at(self, dx, flip):
        yy = 1 - self.y if flip else self.y
        return ((self.x + dx + 4) % 4) * 2 + yy


class Gather:
    def __init__(self, view, rows, send, recv, around):
        self.view, self.rows, self.send, self.recv, self.a = view, rows, send, recv, around
        self.to = {"y": around.at(0, True), "r": around.at(1, False), "l": around.at(-1, False)}

    def op(self, i):
        a, half = self.a, self.rows // 2
        table = [
            ((0, False), (0, True), "y", 0, self.rows),
            ((0, False), (-1, False), "r", 0, self.rows),
            ((0, False), (1, False), "l", 0, self.rows),
            ((0, True), (-1, True), "r", 0, self.rows),
            ((0, True), (1, True), "l", 0, self.rows),
            ((-1, False), (2, False), "r", 0, half),
            ((1, False), (2, False), "l", half, half),
            ((2, False), (2, True), "y", 0, self.rows),
        ]
        src, got, to, first, rows = table[i]
        return a.at(*src), a.at(*got), self.to[to], first, rows

    def copy(self, i, arriving=False, src=None):
        block, got, to, first, rows = self.op(i)
        here = self.view(got if arriving else block, first, rows)
        return remote(here if src is None else src, here, self.send.at[i], self.recv.at[i], ctx=to)

    def start(self, i, src=None):
        self.copy(i, src=src).start()

    def arrived(self, *ops):
        for i in ops:
            self.copy(i, arriving=True).wait_recv()

    def first(self):
        for i in range(3):
            self.start(i)

    def spread(self):
        self.arrived(0)
        self.start(3)
        self.start(4)

    def halves(self):
        self.arrived(1)
        self.start(5)
        self.arrived(2)
        self.start(6)

    def cross(self):
        self.arrived(5, 6)
        self.start(7)

    def finish(self):
        for i in range(8):
            self.copy(i).wait_send()


def layer_kernel(
    q_ref,
    lat_ref,
    ak_ref,
    av_ref,
    wo_ref,
    hid_ref,
    gain_ref,
    mask_ref,
    routes_ref,
    weight_ref,
    perm_ref,
    unperm_ref,
    wg_hbm,
    wu_hbm,
    wd_hbm,
    out_ref,
    gak,
    gav,
    gwo,
    latb,
    qlat,
    sbuf,
    acc,
    mmax,
    lsum,
    attn,
    parts,
    got,
    qb,
    hidb,
    perm,
    unperm,
    wg,
    wu,
    wd,
    xs,
    rx,
    xa,
    pd,
    tb,
    fin,
    ys,
    back,
    own_sem,
    w_send,
    w_recv,
    l_send,
    l_recv,
    r_send,
    r_recv,
    a_send,
    a_recv,
    g_send,
    g_recv,
    s_send,
    s_recv,
    b_send,
    b_recv,
    *,
    scale,
):
    c, e, x, y = place()
    z, h, k = e // 4, (e // 2) % 2, e % 2
    around = Around(x, y)

    def eid(zz, hh, kk):
        return ((zz + 16) % 8) * 4 + hh * 2 + kk

    up, down = eid(z + 1, h, k), eid(z - 1, h, k)
    partner, sibling = eid(z, 1 - h, k), eid(z, h, 1 - k)

    local_copies = [
        pltpu.make_async_copy(src, dst, own_sem.at[i])
        for i, (src, dst) in enumerate(
            (
                (ak_ref, gak.at[e]),
                (lat_ref, latb.at[c, pl.ds(0, MASKED)]),
                (av_ref, gav.at[e]),
                (wo_ref, gwo.at[e]),
                (wg_hbm, wg),
                (wu_hbm, wu),
                (wd_hbm, wd),
                (q_ref, qb),
                (hid_ref, hidb),
                (perm_ref, perm),
                (unperm_ref, unperm),
            )
        )
    ]
    for copy in local_copies[:4] + local_copies[7:8]:
        copy.start()

    barrier = pltpu.get_barrier_semaphore()

    def hello(i, carry):
        pl.semaphore_signal(
            barrier, inc=1, device_id={"exp": (e + i) % NEXP}, device_id_type=MESH
        )
        return carry

    lax.fori_loop(1, NEXP, hello, 0)
    for i in range(1, NCTX):
        pl.semaphore_signal(
            barrier, inc=1, device_id={"ctx": (c + i) % NCTX}, device_id_type=MESH
        )
    pl.semaphore_wait(barrier, NEXP - 1 + NCTX - 1)


    def piece(p, block):
        if p == 0:
            return gak.at[block]
        if p == 3:
            return gav.at[block]
        return gwo.at[block, pl.ds(*PIECE_ROWS[p])]

    def own_piece(p):
        if p == 0:
            return ak_ref
        if p == 3:
            return av_ref
        return wo_ref.at[pl.ds(*PIECE_ROWS[p])]

    def slot(off, flip, other=False):
        return eid(z + off, 1 - h if flip else h, 1 - k if other else k)

    def wcopy(p, ident, block, to, own=False):
        here = piece(p, block)
        return remote(
            own_piece(p) if own else here, here, w_send.at[p, ident], w_recv.at[p, ident], exp=to
        )

    def ring_id(sign, off, flip):
        if off == 4:
            return 7 if sign > 0 else 14
        return (1 if sign > 0 else 8) + (off - 1) * 2 + int(flip)

    def sib_id(off, flip):
        return 16 + (off % 8) * 2 + int(flip)

    started = []

    def send(p, ident, off, flip, to, own=False):
        wcopy(p, ident, slot(off, flip), to, own).start()
        started.append((p, ident, off, flip, to))

    def send_on(p, off, flip, sign, own=False):
        ident = ring_id(sign, off + 1, flip)
        send(p, ident, -sign * off, flip, up if sign > 0 else down, own)

    def send_sibling(p, off, flip, own=False):
        if p == LAST_PIECE:
            p = 5
        if p in (0, 3, 5):
            send(p, sib_id(off, flip), off, flip, sibling, own)

    def weights_first(p):
        for sign in (1, -1):
            send_on(p, 0, False, sign, True)
        send(p, 0, 0, False, partner, True)
        send_sibling(p, 0, False, True)

    def weights_partner(p):
        wcopy(p, 0, slot(0, True), partner).wait_recv()
        for sign in (1, -1):
            send_on(p, 0, True, sign)
        send_sibling(p, 0, True)

    def weights_ring(p, off, flip):
        for sign in (1, -1):
            wcopy(p, ring_id(sign, off, flip), slot(-sign * off, flip), partner).wait_recv()
        for sign in (1, -1):
            if off < 3 or flip == (sign < 0):
                send_on(p, off, flip, sign)
            send_sibling(p, -sign * off, flip)

    def weights_far(p):
        for sign in (1, -1):
            flip = sign < 0
            wcopy(p, ring_id(sign, 4, flip), slot(4, flip), partner).wait_recv()
        for flip in (False, True):
            send_sibling(p, 4, flip)

    def weights_sibling(off, *ps):
        for p in ps:
            for flip in (False, True):
                wcopy(p, sib_id(off, flip), slot(off, flip, True), sibling).wait_recv()

    def latent_view(base):
        return lambda block, first, rows: latb.at[block, pl.ds(base + first, rows)]

    lats = [
        Gather(latent_view(i * HALF_LAT), HALF_LAT, l_send.at[i], l_recv.at[i], around)
        for i in range(2)
    ]

    def latents_first(i):
        for op in range(3):
            lats[i].start(op, lat_ref.at[pl.ds(i * HALF_LAT, HALF_LAT)])

    def prepare():
        for copy in local_copies[4:7] + local_copies[8:]:
            copy.start()
        top = lax.broadcasted_iota(jnp.int32, (16, BLK), 0) == 0

        def fill(i, carry):
            for b in range(CHUNK // BLK):
                cols = slice(b * BLK, (b + 1) * BLK)
                is_open = mask_ref[NCTX * CHUNK // BLK - 1, i * (CHUNK // BLK) + b].astype(F32)
                taken = jnp.where(top, NEG, 0.0) * (1.0 - is_open)
                latb[i, MASKED:CAUSAL, cols] = taken.astype(BF16)
            latb[i, CAUSAL:DEPTH, :] = jnp.zeros((T, CHUNK), BF16)
            return carry

        lax.fori_loop(0, NCTX, fill, 0)
        latb[NCTX - 1, CAUSAL:DEPTH, CHUNK - T : CHUNK] = jnp.where(lane > sub, NEG, 0.0).astype(BF16)
        ones = jnp.where(lane[:, 0:16] == 0, 1.0, 0.0).astype(BF16)
        for head in range(HL):
            qlat[head * T : (head + 1) * T, MASKED:CAUSAL] = ones
            qlat[head * T : (head + 1) * T, CAUSAL:DEPTH] = eye

    sub = lax.broadcasted_iota(jnp.int32, (T, T), 0)
    lane = lax.broadcasted_iota(jnp.int32, (T, T), 1)
    eye = jnp.where(sub == lane, 1.0, 0.0).astype(BF16)

    def column(row):
        return jnp.sum(jnp.where(sub == lane, row, 0.0), axis=1, keepdims=True)

    def places():
        earlier = jnp.where(sub < lane, 1.0, 0.0).astype(BF16)
        expert_of_row = sub.astype(F32)
        routes = [routes_ref[i : i + 1, :].astype(F32) for i in range(TOPK)]
        named = [jnp.where(expert_of_row == r, 1.0, 0.0) for r in routes]
        before = dot((named[0] + named[1]).astype(BF16), earlier)
        return [
            r * 4 + jnp.sum(before * n, axis=0, keepdims=True)
            for r, n in zip(routes, named, strict=True)
        ]

    def absorb():
        for off in range(8):
            weights_sibling(off, 0)
        for copy in local_copies[:4] + local_copies[7:8]:
            copy.wait()

        def body(i, carry):
            pair_q = qb[:, pl.ds(pl.multiple_of(i * 384, 384), 384)]
            for j in range(2):
                at = j * (DN + DR)
                rows = pl.ds(pl.multiple_of(i * 2 * T + j * T, T), T)
                weight = gak[:, pl.ds(i * 2 + j, 1)].reshape(DC, DN)
                qlat[rows, 0:DC] = (dot(pair_q[:, at : at + DN], weight, NT) * factor).astype(BF16)
                rope = pair_q[:, at + DN : at + DN + DR].astype(F32) * factor
                qlat[rows, DC : DC + DR] = rope.astype(BF16)
            return carry

        lax.fori_loop(0, HL // 2, body, 0)

    factor = scale * math.log2(math.e)
    groups = [
        [around.at(0, False), around.at(0, True)],
        [around.at(-1, False), around.at(1, False)],
        [around.at(2, False), around.at(-1, True)],
        [around.at(1, True), around.at(2, True)],
    ]
    step_rows = HL * T // 4

    def score(g, q):
        rows = pl.ds(q * step_rows, step_rows)
        for i, b in enumerate(groups[g]):
            sbuf[q % 2, i] = dot(qlat[rows, :], latb[b])

    def attend(g, q):
        if q == 0:
            for piece_of in lats:
                if g == 2:
                    piece_of.arrived(3)
                if g == 3:
                    piece_of.arrived(4, 7)
            score(g, 0)
        if q < 3:
            score(g, q + 1)
        rows = pl.ds(q * step_rows, step_rows)
        scores = [sbuf[q % 2, i] for i in range(2)]
        top = jnp.max(jnp.maximum(*scores), axis=1, keepdims=True)
        if g > 0:
            old = mmax[rows, 0:1]
            top = jnp.maximum(old, top)
        probs = [jnp.exp2(s - top) for s in scores]
        total = jnp.sum(probs[0] + probs[1], axis=1, keepdims=True)
        product = sum(
            dot(p.astype(BF16), latb[b, 0:DC, :], NT)
            for p, b in zip(probs, groups[g], strict=True)
        )
        if g > 0:
            shrink = jnp.exp2(old - top)
            total = total + lsum[rows, 0:1] * shrink
            product = product + acc[rows, :] * shrink
        mmax[rows, :] = jnp.broadcast_to(top, (step_rows, 128))
        lsum[rows, :] = jnp.broadcast_to(total, (step_rows, 128))
        acc[rows, :] = product

    def values():
        for off in range(8):
            weights_sibling(off, 3)

        def body(head, carry):
            cols = pl.ds(pl.multiple_of(head * DV, DV), DV)
            rows = pl.ds(pl.multiple_of(head * T, T), T)
            weight = gav[:, pl.ds(head, 1)].reshape(DC, DV)
            latent_out = (acc[rows, :] * (1.0 / lsum[rows, 0:1])).astype(BF16)
            attn[:, cols] = dot(latent_out, weight).astype(BF16)
            return carry

        lax.fori_loop(0, HL, body, 0)


    def rcopy(dest, source):
        return remote(parts.at[dest], got.at[source], r_send.at[dest], r_recv.at[source], ctx=dest)

    def project(off):
        weights_sibling(off, 5)
        dest = (z + off + 8) % 8
        weight = gwo[pl.ds(dest * 4, 4)].reshape(SHARE, HL * DV)
        partial = dot(attn[...], weight, NT)
        parts[dest, :, 0:SHARE] = partial.astype(BF16)
        parts[dest, :, SHARE:WIDE] = jnp.zeros((T, WIDE - SHARE), BF16)

        @pl.when(dest != c)
        def _():
            rcopy(dest, c).start()

        @pl.when(dest == c)
        def _():
            got[c] = parts[dest]

    acts = {
        "first": weights_first,
        "partner": weights_partner,
        "ring": weights_ring,
        "far": weights_far,
        "latents": latents_first,
        "spread": lambda i: lats[i].spread(),
        "halves": lambda i: lats[i].halves(),
        "cross": lambda i: lats[i].cross(),
        "prepare": prepare,
        "absorb": absorb,
        "attend": attend,
        "values": values,
        "project": project,
    }
    for act, *how in PLAN:
        acts[act](*how)
    place_rows = places()
    place_cols = [column(r) for r in place_rows]

    for i in range(1, NCTX):
        source = (c + i) % NCTX
        here = got.at[source]
        remote(here, here, r_send.at[source], r_recv.at[source], ctx=source).wait_recv()
    for copy in local_copies[4:7] + local_copies[8:]:
        copy.wait()
    resid = dot(eye, hidb[...], NT)
    for i in range(NCTX):
        resid = resid + got[i, :, 0:SHARE].astype(F32)

    squares = jnp.sum(resid * resid, axis=1, keepdims=True)
    high = squares.astype(BF16).astype(F32)
    low = squares - high
    beside = lax.broadcasted_iota(jnp.int32, (T, WIDE - SHARE), 1)
    tail = jnp.where(beside == 0, high, jnp.where(beside == 1, low, 0.0))
    gains = jnp.concatenate([gain_ref[pl.ds(x * 7 + i, 1), :] for i in range(7)], axis=1)
    gain = jnp.where(y == 0, gains[:, 0:SHARE], gains[:, SHARE:])
    scaled = jnp.concatenate([resid * gain, tail], axis=1).astype(BF16)
    where = lax.broadcasted_iota(jnp.int32, (GRID, T), 0).astype(F32)
    chosen = (where == place_rows[0]) | (where == place_rows[1])
    xs[...] = dot(jnp.where(chosen, 1.0, 0.0).astype(BF16), scaled).astype(BF16)

    def rows16(i):
        return pl.ds(pl.multiple_of(i * 16, 16), 16)

    def exchange(src, dst, send_sem, recv_sem):
        def make(i):
            to = (e + i) % NEXP
            return remote(
                src.at[rows16(to)], dst.at[rows16(e)], send_sem.at[i], recv_sem.at[i], exp=to
            )

        def go(i, carry):
            make(i).start()
            return carry

        def land(i, carry):
            frm = (e + NEXP - i) % NEXP
            here = dst.at[rows16(frm)]
            remote(here, here, send_sem.at[i], recv_sem.at[i], exp=frm).wait_recv()
            return carry

        def left(i, carry):
            make(i).wait_send()
            return carry

        lax.fori_loop(1, NEXP, go, 0)
        dst[rows16(e), :] = src[rows16(e), :]
        lax.fori_loop(1, NEXP, land, 0)
        return lambda: lax.fori_loop(1, NEXP, left, 0)

    a_left = exchange(xs, rx, a_send, a_recv)
    for j in range(4):
        xa[c, j] = dot(perm[j * ROWS : (j + 1) * ROWS, :], rx[...]).astype(BF16)

    def rows_view(j):
        return lambda block, first, rows: xa.at[block, j, pl.ds(first, rows)]

    gathers = [Gather(rows_view(j), ROWS, g_send.at[j], g_recv.at[j], around) for j in range(4)]
    for g in gathers:
        g.first()

    lanes = lax.broadcasted_iota(jnp.int32, (ROWS, 128), 1)

    def expert(j):
        gathers[j].arrived(3, 4, 7)

        def feed(block, carry):
            g, u, t = carry
            rows_c = pl.ds(pl.multiple_of(block * SHARE, SHARE), SHARE)
            lhs = xa[block, j, :, 0:SHARE]
            g = g + dot(lhs, wg[j, rows_c, :])
            u = u + dot(lhs, wu[j, rows_c, :])
            return g, u, t + xa[block, j, :, 384:WIDE].astype(F32)

        zero = jnp.zeros((ROWS, FFL), F32)
        g, u, t = lax.fori_loop(0, NCTX, feed, (zero, zero, zero))
        kept = jnp.where((lanes == 64) | (lanes == 65), t, 0.0)
        inv = lax.rsqrt(jnp.sum(kept, axis=1, keepdims=True) / D + 1e-06)
        g, u = g * inv, u * inv
        act = (g / (1.0 + jnp.exp(-g)) * u).astype(BF16)

        def produce(xx, carry):
            cols = pl.ds(pl.multiple_of(xx * 2 * SHARE, 2 * SHARE), 2 * SHARE)
            both = dot(act, wd[j, :, cols]).astype(BF16)
            blank = jnp.zeros((ROWS, WIDE - SHARE), BF16)
            pd[xx * 2, j, :, 0:SHARE] = both[:, 0:SHARE]
            pd[xx * 2 + 1, j, :, 0:SHARE] = both[:, SHARE:]
            pd[xx * 2, j, :, SHARE:WIDE] = blank
            pd[xx * 2 + 1, j, :, SHARE:WIDE] = blank
            return carry

        lax.fori_loop(0, NCTX // 2, produce, 0)
        for i in (0, 1, 2, 6, 7):
            scopy(j, i).start()

    half = ROWS // 2
    lo, hi, whole = pl.ds(0, half), pl.ds(half, half), pl.ds(0, ROWS)
    yp, xr, xl = around.at(0, True), around.at(1, False), around.at(-1, False)
    sends = [
        (around.at(2, True), whole, 0, yp),
        (around.at(1, True), whole, 1, xr),
        (around.at(-1, True), whole, 2, xl),
        (around.at(2, False), lo, 3, xr),
        (around.at(2, False), hi, 4, xl),
        (around.at(0, True), whole, 5, yp),
        (around.at(1, False), hi, 6, xr),
        (around.at(-1, False), lo, 7, xl),
        (around.at(1, False), lo, 6, xr),
        (around.at(-1, False), hi, 7, xl),
    ]

    def scopy(j, i):
        block, rows, land, to = sends[i]
        return remote(
            pd.at[block, j, rows], tb.at[land, j, rows], s_send.at[j, i], s_recv.at[j, i], ctx=to
        )

    def sgot(j, *ops):
        for i in ops:
            _, rows, land, to = sends[i]
            here = tb.at[land, j, rows]
            remote(here, here, s_send.at[j, i], s_recv.at[j, i], ctx=to).wait_recv()

    def add(j, block, rows, *lands):
        total = pd[block, j, rows, :].astype(F32)
        for land in lands:
            total = total + tb[land, j, rows, :].astype(F32)
        pd[block, j, rows, :] = total.astype(BF16)

    def reduce1(j):
        sgot(j, 0)
        add(j, around.at(2, False), whole, 0)
        scopy(j, 3).start()
        scopy(j, 4).start()
        sgot(j, 1, 2)
        add(j, around.at(0, True), whole, 1, 2)
        scopy(j, 5).start()

    def reduce2(j):
        sgot(j, 3)
        add(j, around.at(1, False), lo, 3)
        scopy(j, 8).start()
        sgot(j, 4)
        add(j, around.at(-1, False), hi, 4)
        scopy(j, 9).start()

    def reduce3(j):
        sgot(j, 5, 6, 7, 8, 9)
        total = pd[c, j].astype(F32)
        for land in (5, 6, 7):
            total = total + tb[land, j].astype(F32)
        fin[j * ROWS : (j + 1) * ROWS, :] = total.astype(BF16)

    gathers[0].spread()
    gathers[0].halves()
    gathers[1].spread()
    gathers[1].halves()
    gathers[0].cross()
    gathers[2].spread()
    gathers[2].halves()
    gathers[3].spread()
    gathers[3].halves()
    gathers[1].cross()
    expert(0)
    gathers[2].cross()
    gathers[3].cross()
    expert(1)
    reduce1(0)
    expert(2)
    reduce1(1)
    reduce2(0)
    expert(3)
    reduce1(2)
    reduce2(1)
    reduce3(0)
    reduce1(3)
    reduce2(2)
    reduce3(1)
    reduce2(3)
    reduce3(2)
    reduce3(3)
    ys[...] = dot(unperm[...], fin[...]).astype(BF16)

    b_left = exchange(ys, back, b_send, b_recv)
    spots = lax.broadcasted_iota(jnp.int32, (T, GRID), 1).astype(F32)
    result = resid
    for i in range(TOPK):
        picked = jnp.where(spots == place_cols[i], 1.0, 0.0).astype(BF16)
        result = result + dot(picked, back[...])[:, 0:SHARE] * column(weight_ref[i : i + 1, :])
    out_ref[...] = result.astype(BF16)

    for p, ident, off, flip, to in started:
        wcopy(p, ident, slot(off, flip), to).wait_send()
    for g in lats + gathers:
        g.finish()
    for i in range(1, NCTX):
        rcopy((c + i) % NCTX, c).wait_send()
    for j in range(4):
        for i in range(10):
            scopy(j, i).wait_send()
    a_left()
    b_left()


def permutations():
    perm = np.zeros((SLOTS, GRID), np.float32)
    for j in range(4):
        for s in range(NEXP):
            for i in range(3):
                perm[j * ROWS + s * 3 + i, s * 16 + j * 4 + i] = 1.0
    return perm


VMEM = pl.BlockSpec(memory_space=pltpu.VMEM)
SMEM = pl.BlockSpec(memory_space=pltpu.SMEM)
ANY = pl.BlockSpec(memory_space=pl.ANY)


def local(
    query,
    latent_cache,
    absorb_key,
    absorb_value,
    out_weight,
    hidden,
    norm_gain,
    block_mask,
    routes,
    route_weight,
    w_gate,
    w_up,
    w_down,
):
    perm = permutations()
    dma = pltpu.SemaphoreType.DMA
    return pl.pallas_call(
        functools.partial(layer_kernel, scale=1.0 / math.sqrt(DN + DR)),
        out_shape=jax.ShapeDtypeStruct((T, SHARE), BF16),
        in_specs=[ANY] * 6 + [VMEM, SMEM, VMEM, VMEM] + [ANY] * 5,
        out_specs=VMEM,
        scratch_shapes=[
            pltpu.VMEM((NEXP, HL, 16, DN), BF16),
            pltpu.VMEM((NEXP, HL, 16, DV), BF16),
            pltpu.VMEM((NEXP, WO, HL * DV), BF16),
            pltpu.VMEM((NCTX, DEPTH, CHUNK), BF16),
            pltpu.VMEM((HL * T, DEPTH), BF16),
            pltpu.VMEM((2, 2, HL * T // 4, CHUNK), F32),
            pltpu.VMEM((HL * T, DC), F32),
            pltpu.VMEM((HL * T, 128), F32),
            pltpu.VMEM((HL * T, 128), F32),
            pltpu.VMEM((T, HL * DV), BF16),
            pltpu.VMEM((NCTX, T, WIDE), BF16),
            pltpu.VMEM((NCTX, T, WIDE), BF16),
            pltpu.VMEM((T, HL * (DN + DR)), BF16),
            pltpu.VMEM((SHARE, T), BF16),
            pltpu.VMEM((SLOTS, GRID), BF16),
            pltpu.VMEM((GRID, SLOTS), BF16),
            pltpu.VMEM((4, D, FFL), BF16),
            pltpu.VMEM((4, D, FFL), BF16),
            pltpu.VMEM((4, FFL, D), BF16),
            pltpu.VMEM((GRID, WIDE), BF16),
            pltpu.VMEM((GRID, WIDE), BF16),
            pltpu.VMEM((NCTX, 4, ROWS, WIDE), BF16),
            pltpu.VMEM((NCTX, 4, ROWS, WIDE), BF16),
            pltpu.VMEM((8, 4, ROWS, WIDE), BF16),
            pltpu.VMEM((SLOTS, WIDE), BF16),
            pltpu.VMEM((GRID, WIDE), BF16),
            pltpu.VMEM((GRID, WIDE), BF16),
            dma((11,)),
            dma((6, 32)),
            dma((6, 32)),
            dma((2, 8)),
            dma((2, 8)),
            dma((NCTX,)),
            dma((NCTX,)),
            dma((NEXP,)),
            dma((NEXP,)),
            dma((4, 8)),
            dma((4, 8)),
            dma((4, 10)),
            dma((4, 10)),
            dma((NEXP,)),
            dma((NEXP,)),
        ],
        compiler_params=pltpu.CompilerParams(
            collective_id=0, has_side_effects=True, vmem_limit_bytes=54 * 1024 * 1024
        ),
        name="layer",
    )(
        query,
        latent_cache[0].T,
        absorb_key.transpose(0, 2, 1),
        absorb_value,
        out_weight.T,
        hidden.T,
        norm_gain.reshape(D // 128, 128),
        block_mask,
        routes.T,
        route_weight.T,
        jnp.asarray(perm, BF16),
        jnp.asarray(perm.T, BF16),
        w_gate,
        w_up,
        w_down,
    )


def solution(mesh):
    in_specs = (
        P("exp", "ctx"),
        P("exp", "ctx", None),
        P("ctx", None, "exp"),
        P("ctx", "exp", None),
        P("ctx", "exp"),
        P("exp", "ctx"),
        P(),
        P(),
        P("exp", None),
        P("exp", None),
        P("exp", None, "ctx"),
        P("exp", None, "ctx"),
        P("exp", "ctx", None),
    )
    out_specs = P("exp", "ctx")
    return jax.shard_map(local, mesh=mesh, in_specs=in_specs, out_specs=out_specs, check_vma=False)
```

time: 819 us -> 167 us (0.20)
  waiting for transfers between devices: 565 us -> 0 us
  Pallas kernels: 0 us -> 165 us
  blocking collectives: 77 us -> 0 us
  local copies, waits for them, and re-layouts: 77.6 us -> 1.67 us
  matrix products: 48.6 us -> 0 us
  other arithmetic: 24.7 us -> 0 us
  between operations: 14 us -> 0.01 us
    all_gather x4 -> x0, waiting for transfers between devices: 302 us -> none  [the longest x1 111 us: local(): rows_here = lax.all_gather(latent_cache, 'ctx', axis=1, tiled=True)[0]]
    pallas_call x0 -> x1, Pallas kernels: none -> 165 us  [local(): pl.pallas_call(functools.partial(layer_kernel, scale=1.0 / math.sqrt(DN +...]
    all_to_all x1 -> x0, waiting for transfers between devices: 125 us -> none  [local(): lax.all_to_all(produced, 'exp', split_axis=0, concat_axis=0, tiled=True)]
    psum x1 -> x0, waiting for transfers between devices: 92.9 us -> none  [local(): residual = lax.psum(partial_value + placed, 'ctx')]
    all_to_all x1 -> x0, blocking collectives: 77 us -> none  [local(): lax.all_to_all(outgoing, 'exp', split_axis=0, concat_axis=0, tiled=True)]
    dot_general x6 -> x0, matrix products: 48.6 us -> none  [the longest x1 12.1 us: local(): jnp.einsum('qhc,hcv->qhv', latent_out, absorb_value, preferred_element_ty...]
    unnamed x7 -> x0, waiting for transfers between devices: 45.3 us -> none
    gather x3 -> x0, local copies, waits for them, and re-layouts: 24 us -> none  [the longest x2 13.3 us: local(): row_out = returned.reshape(expert_total * capacity, width_back)[destination]]
  transfers between devices with their start and end apart: 7 -> 0, of which waited for: 7 -> 0; matrix products, arithmetic and copies ran while one was open for 8% -> 0% of each run, Pallas kernels for 0% -> 0%
where the time goes in v2:
time: 167 us; the launch traced here: 166 us
  Pallas kernels  165 us (99%)
  local copies, waits for them, and re-layouts  1.67 us (1%)
    pallas_call x1, Pallas kernels, local(): pl.pallas_call(functools.partial(layer_kernel, scale=1.0 / math.sqrt(DN +...  165 us

profile of v2, /device:TPU:1, one launch (start us, length us, event | category | flops | bytes accessed | tf_op | source)
XLA Modules:
  0.0 166.4 jit_solution(14284212702386531960)
XLA Ops:
  0.0 164.7 %layer.1 = bf16[128,448]{1,0:T(8,128)(2,1)} custom-call(bf16[128,1536]{1,0:T(8,128)(2,1)} %q_ref.1, bf16[576,512]{1,0:T(8,128)(2,1)} %bitcast.9, bf16[8,16,128]{2,1,0:T(8,128)(2,1)} %bitcast.12, bf16[8,16,128]{2,1,0:T(8,128)(2,1)} %av_ref.1, bf16[112,1024]{1,0:T(8,128)(2,1)} %bitcast.10, bf16[448,128]{1,0:T(8,128)(2,1)} %bitcast.11, f32[28,128]{1,0:T(8,128)} %bitcast.13, ...), custom_call_target="tpu_custom_call" | custom-call | tf_op jit(solution)/shard_map/layer/pallas_call | solution.py:735
  164.7 1.7 %copy.16 = bf16[128,448]{0,1:T(8,128)(2,1)} copy(bf16[128,448]{1,0:T(8,128)(2,1)} %layer.1) | data formatting | bytes 229376 | tf_op jit(solution)/shard_map/layer/pallas_call | solution.py:735

commit v3 on v2

--- a/solution.py
+++ b/solution.py
@@ -85,6 +85,9 @@
 
 
 class Gather:
+    GROUP = (0, 1, 1, 3, 4, 2, 2, 4)
+    BLOCKS = (1, 2, 1, 1, 2)
+
     def __init__(self, view, rows, send, recv, around):
         self.view, self.rows, self.send, self.recv, self.a = view, rows, send, recv, around
         self.to = {"y": around.at(0, True), "r": around.at(1, False), "l": around.at(-1, False)}
@@ -104,17 +107,16 @@
         src, got, to, first, rows = table[i]
         return a.at(*src), a.at(*got), self.to[to], first, rows
 
-    def copy(self, i, arriving=False, src=None):
-        block, got, to, first, rows = self.op(i)
-        here = self.view(got if arriving else block, first, rows)
-        return remote(here if src is None else src, here, self.send.at[i], self.recv.at[i], ctx=to)
-
     def start(self, i, src=None):
-        self.copy(i, src=src).start()
-
-    def arrived(self, *ops):
-        for i in ops:
-            self.copy(i, arriving=True).wait_recv()
+        block, _, to, first, rows = self.op(i)
+        here = self.view(block, first, rows)
+        group = self.GROUP[i]
+        remote(here if src is None else src, here, self.send, self.recv.at[group], ctx=to).start()
+
+    def arrived(self, group):
+        blocks = self.BLOCKS[group]
+        here = self.view(pl.ds(0, blocks), 0, self.rows)
+        remote(here, here, self.send, self.recv.at[group], ctx=self.to["y"]).wait_recv()
 
     def first(self):
         for i in range(3):
@@ -128,16 +130,11 @@
     def halves(self):
         self.arrived(1)
         self.start(5)
+        self.start(6)
+
+    def cross(self):
         self.arrived(2)
-        self.start(6)
-
-    def cross(self):
-        self.arrived(5, 6)
         self.start(7)
-
-    def finish(self):
-        for i in range(8):
-            self.copy(i).wait_send()
 
 
 def layer_kernel(
@@ -147,10 +144,10 @@
     av_ref,
     wo_ref,
     hid_ref,
-    gain_ref,
-    mask_ref,
-    routes_ref,
-    weight_ref,
+    gain_hbm,
+    mask_hbm,
+    routes_hbm,
+    weight_hbm,
     perm_ref,
     unperm_ref,
     wg_hbm,
@@ -171,6 +168,10 @@
     got,
     qb,
     hidb,
+    gain_ref,
+    mask_ref,
+    routes_ref,
+    weight_ref,
     perm,
     unperm,
     wg,
@@ -187,18 +188,17 @@
     own_sem,
     w_send,
     w_recv,
+    sib_recv,
     l_send,
     l_recv,
     r_send,
     r_recv,
-    a_send,
-    a_recv,
+    a_sems,
     g_send,
     g_recv,
     s_send,
     s_recv,
-    b_send,
-    b_recv,
+    b_sems,
     *,
     scale,
 ):
@@ -227,11 +227,16 @@
                 (hid_ref, hidb),
                 (perm_ref, perm),
                 (unperm_ref, unperm),
+                (mask_hbm, mask_ref),
+                (gain_hbm, gain_ref),
+                (routes_hbm, routes_ref),
+                (weight_hbm, weight_ref),
             )
         )
     ]
-    for copy in local_copies[:4] + local_copies[7:8]:
-        copy.start()
+    early = local_copies[:4] + [local_copies[7]]
+    mask_copy = local_copies[11]
+    late = local_copies[4:7] + local_copies[8:11] + local_copies[12:]
 
     barrier = pltpu.get_barrier_semaphore()
 
@@ -246,6 +251,8 @@
         pl.semaphore_signal(
             barrier, inc=1, device_id={"ctx": (c + i) % NCTX}, device_id_type=MESH
         )
+    for copy in early + [mask_copy]:
+        copy.start()
     pl.semaphore_wait(barrier, NEXP - 1 + NCTX - 1)
 
 
@@ -266,73 +273,69 @@
     def slot(off, flip, other=False):
         return eid(z + off, 1 - h if flip else h, 1 - k if other else k)
 
-    def wcopy(p, ident, block, to, own=False):
-        here = piece(p, block)
-        return remote(
-            own_piece(p) if own else here, here, w_send.at[p, ident], w_recv.at[p, ident], exp=to
-        )
-
-    def ring_id(sign, off, flip):
-        if off == 4:
-            return 7 if sign > 0 else 14
-        return (1 if sign > 0 else 8) + (off - 1) * 2 + int(flip)
-
-    def sib_id(off, flip):
-        return 16 + (off % 8) * 2 + int(flip)
-
-    started = []
-
-    def send(p, ident, off, flip, to, own=False):
-        wcopy(p, ident, slot(off, flip), to, own).start()
-        started.append((p, ident, off, flip, to))
+    def group_of(p):
+        return {0: 0, 3: 1}.get(p, 2)
+
+    def wcopy(p, ref, sem, to, src=None):
+        return remote(ref if src is None else src, ref, w_send.at[group_of(p)], sem, exp=to)
+
+    def ring_sem(p, off, flip):
+        return w_recv.at[p, 7 if off == 4 else 1 + (off - 1) * 2 + int(flip)]
+
+    def sibling_sem(p, off):
+        return sib_recv.at[off % 8 + 2] if p == 5 else sib_recv.at[group_of(p)]
 
     def send_on(p, off, flip, sign, own=False):
-        ident = ring_id(sign, off + 1, flip)
-        send(p, ident, -sign * off, flip, up if sign > 0 else down, own)
+        here = piece(p, slot(-sign * off, flip))
+        src = own_piece(p) if own else None
+        wcopy(p, here, ring_sem(p, off + 1, flip), up if sign > 0 else down, src).start()
 
     def send_sibling(p, off, flip, own=False):
         if p == LAST_PIECE:
             p = 5
         if p in (0, 3, 5):
-            send(p, sib_id(off, flip), off, flip, sibling, own)
+            here = piece(p, slot(off, flip))
+            wcopy(p, here, sibling_sem(p, off), sibling, own_piece(p) if own else None).start()
+
+    def pieces(p, count):
+        if p == 0:
+            return gak.at[pl.ds(0, count)]
+        if p == 3:
+            return gav.at[pl.ds(0, count)]
+        return gwo.at[pl.ds(0, count), pl.ds(*PIECE_ROWS[p])]
 
     def weights_first(p):
         for sign in (1, -1):
             send_on(p, 0, False, sign, True)
-        send(p, 0, 0, False, partner, True)
+        wcopy(p, piece(p, e), w_recv.at[p, 0], partner, own_piece(p)).start()
         send_sibling(p, 0, False, True)
 
     def weights_partner(p):
-        wcopy(p, 0, slot(0, True), partner).wait_recv()
+        wcopy(p, pieces(p, 1), w_recv.at[p, 0], partner).wait_recv()
         for sign in (1, -1):
             send_on(p, 0, True, sign)
         send_sibling(p, 0, True)
 
     def weights_ring(p, off, flip):
-        for sign in (1, -1):
-            wcopy(p, ring_id(sign, off, flip), slot(-sign * off, flip), partner).wait_recv()
+        wcopy(p, pieces(p, 2), ring_sem(p, off, flip), partner).wait_recv()
         for sign in (1, -1):
             if off < 3 or flip == (sign < 0):
                 send_on(p, off, flip, sign)
             send_sibling(p, -sign * off, flip)
 
     def weights_far(p):
-        for sign in (1, -1):
-            flip = sign < 0
-            wcopy(p, ring_id(sign, 4, flip), slot(4, flip), partner).wait_recv()
+        wcopy(p, pieces(p, 2), ring_sem(p, 4, False), partner).wait_recv()
         for flip in (False, True):
             send_sibling(p, 4, flip)
 
-    def weights_sibling(off, *ps):
-        for p in ps:
-            for flip in (False, True):
-                wcopy(p, sib_id(off, flip), slot(off, flip, True), sibling).wait_recv()
+    def weights_sibling(p, off, count):
+        wcopy(p, pieces(p, count), sibling_sem(p, off), sibling).wait_recv()
 
     def latent_view(base):
         return lambda block, first, rows: latb.at[block, pl.ds(base + first, rows)]
 
     lats = [
-        Gather(latent_view(i * HALF_LAT), HALF_LAT, l_send.at[i], l_recv.at[i], around)
+        Gather(latent_view(i * HALF_LAT), HALF_LAT, l_send.at[0], l_recv.at[i], around)
         for i in range(2)
     ]
 
@@ -341,14 +344,19 @@
             lats[i].start(op, lat_ref.at[pl.ds(i * HALF_LAT, HALF_LAT)])
 
     def prepare():
-        for copy in local_copies[4:7] + local_copies[8:]:
+        for copy in late:
             copy.start()
+        mask_copy.wait()
+        blocks = NCTX * CHUNK // BLK
+        last = mask_ref[blocks - 1 : blocks, :].astype(F32)
+        at = lax.broadcasted_iota(jnp.int32, (1, blocks), 1)
         top = lax.broadcasted_iota(jnp.int32, (16, BLK), 0) == 0
 
         def fill(i, carry):
             for b in range(CHUNK // BLK):
                 cols = slice(b * BLK, (b + 1) * BLK)
-                is_open = mask_ref[NCTX * CHUNK // BLK - 1, i * (CHUNK // BLK) + b].astype(F32)
+                here = at == i * (CHUNK // BLK) + b
+                is_open = jnp.sum(jnp.where(here, last, 0.0), axis=1, keepdims=True)
                 taken = jnp.where(top, NEG, 0.0) * (1.0 - is_open)
                 latb[i, MASKED:CAUSAL, cols] = taken.astype(BF16)
             latb[i, CAUSAL:DEPTH, :] = jnp.zeros((T, CHUNK), BF16)
@@ -380,9 +388,8 @@
         ]
 
     def absorb():
-        for off in range(8):
-            weights_sibling(off, 0)
-        for copy in local_copies[:4] + local_copies[7:8]:
+        weights_sibling(0, 0, 16)
+        for copy in early:
             copy.wait()
 
         def body(i, carry):
@@ -418,7 +425,7 @@
                 if g == 2:
                     piece_of.arrived(3)
                 if g == 3:
-                    piece_of.arrived(4, 7)
+                    piece_of.arrived(4)
             score(g, 0)
         if q < 3:
             score(g, q + 1)
@@ -443,8 +450,7 @@
         acc[rows, :] = product
 
     def values():
-        for off in range(8):
-            weights_sibling(off, 3)
+        weights_sibling(3, 0, 16)
 
         def body(head, carry):
             cols = pl.ds(pl.multiple_of(head * DV, DV), DV)
@@ -458,10 +464,10 @@
 
 
     def rcopy(dest, source):
-        return remote(parts.at[dest], got.at[source], r_send.at[dest], r_recv.at[source], ctx=dest)
+        return remote(parts.at[dest], got.at[source], r_send.at[0], r_recv.at[0], ctx=dest)
 
     def project(off):
-        weights_sibling(off, 5)
+        weights_sibling(5, off, 2)
         dest = (z + off + 8) % 8
         weight = gwo[pl.ds(dest * 4, 4)].reshape(SHARE, HL * DV)
         partial = dot(attn[...], weight, NT)
@@ -493,15 +499,13 @@
     }
     for act, *how in PLAN:
         acts[act](*how)
+
+    here = got.at[pl.ds(0, NCTX - 1)]
+    remote(here, here, r_send.at[0], r_recv.at[0], ctx=around.at(0, True)).wait_recv()
+    for copy in late:
+        copy.wait()
     place_rows = places()
     place_cols = [column(r) for r in place_rows]
-
-    for i in range(1, NCTX):
-        source = (c + i) % NCTX
-        here = got.at[source]
-        remote(here, here, r_send.at[source], r_recv.at[source], ctx=source).wait_recv()
-    for copy in local_copies[4:7] + local_copies[8:]:
-        copy.wait()
     resid = dot(eye, hidb[...], NT)
     for i in range(NCTX):
         resid = resid + got[i, :, 0:SHARE].astype(F32)
@@ -521,47 +525,36 @@
     def rows16(i):
         return pl.ds(pl.multiple_of(i * 16, 16), 16)
 
-    def exchange(src, dst, send_sem, recv_sem):
-        def make(i):
+    def exchange(src, dst, sems):
+        def go(i, carry):
             to = (e + i) % NEXP
-            return remote(
-                src.at[rows16(to)], dst.at[rows16(e)], send_sem.at[i], recv_sem.at[i], exp=to
-            )
-
-        def go(i, carry):
-            make(i).start()
-            return carry
-
-        def land(i, carry):
-            frm = (e + NEXP - i) % NEXP
-            here = dst.at[rows16(frm)]
-            remote(here, here, send_sem.at[i], recv_sem.at[i], exp=frm).wait_recv()
-            return carry
-
-        def left(i, carry):
-            make(i).wait_send()
+            here, there = src.at[rows16(to)], dst.at[rows16(e)]
+            remote(here, there, sems.at[0], sems.at[1], exp=to).start()
             return carry
 
         lax.fori_loop(1, NEXP, go, 0)
         dst[rows16(e), :] = src[rows16(e), :]
-        lax.fori_loop(1, NEXP, land, 0)
-        return lambda: lax.fori_loop(1, NEXP, left, 0)
-
-    a_left = exchange(xs, rx, a_send, a_recv)
+        everything = pl.ds(0, (NEXP - 1) * 16)
+        all_sent = remote(src.at[everything], dst.at[everything], sems.at[0], sems.at[1], exp=sibling)
+        all_sent.wait_recv()
+        return all_sent
+
+    a_left = exchange(xs, rx, a_sems)
     for j in range(4):
         xa[c, j] = dot(perm[j * ROWS : (j + 1) * ROWS, :], rx[...]).astype(BF16)
 
     def rows_view(j):
         return lambda block, first, rows: xa.at[block, j, pl.ds(first, rows)]
 
-    gathers = [Gather(rows_view(j), ROWS, g_send.at[j], g_recv.at[j], around) for j in range(4)]
+    gathers = [Gather(rows_view(j), ROWS, g_send.at[0], g_recv.at[j], around) for j in range(4)]
     for g in gathers:
         g.first()
 
     lanes = lax.broadcasted_iota(jnp.int32, (ROWS, 128), 1)
 
     def expert(j):
-        gathers[j].arrived(3, 4, 7)
+        gathers[j].arrived(3)
+        gathers[j].arrived(4)
 
         def feed(block, carry):
             g, u, t = carry
@@ -608,17 +601,17 @@
         (around.at(-1, False), hi, 7, xl),
     ]
 
+    groups_of = (0, 1, 1, 2, 2, 3, 3, 3, 3, 3)
+    whole_blocks = (1, 2, 1, 3)
+
     def scopy(j, i):
         block, rows, land, to = sends[i]
-        return remote(
-            pd.at[block, j, rows], tb.at[land, j, rows], s_send.at[j, i], s_recv.at[j, i], ctx=to
-        )
-
-    def sgot(j, *ops):
-        for i in ops:
-            _, rows, land, to = sends[i]
-            here = tb.at[land, j, rows]
-            remote(here, here, s_send.at[j, i], s_recv.at[j, i], ctx=to).wait_recv()
+        here, there = pd.at[block, j, rows], tb.at[land, j, rows]
+        return remote(here, there, s_send.at[0], s_recv.at[j, groups_of[i]], ctx=to)
+
+    def sgot(j, group):
+        here = tb.at[pl.ds(0, whole_blocks[group]), j]
+        remote(here, here, s_send.at[0], s_recv.at[j, group], ctx=yp).wait_recv()
 
     def add(j, block, rows, *lands):
         total = pd[block, j, rows, :].astype(F32)
@@ -631,20 +624,19 @@
         add(j, around.at(2, False), whole, 0)
         scopy(j, 3).start()
         scopy(j, 4).start()
-        sgot(j, 1, 2)
+        sgot(j, 1)
         add(j, around.at(0, True), whole, 1, 2)
         scopy(j, 5).start()
 
     def reduce2(j):
-        sgot(j, 3)
+        sgot(j, 2)
         add(j, around.at(1, False), lo, 3)
         scopy(j, 8).start()
-        sgot(j, 4)
         add(j, around.at(-1, False), hi, 4)
         scopy(j, 9).start()
 
     def reduce3(j):
-        sgot(j, 5, 6, 7, 8, 9)
+        sgot(j, 3)
         total = pd[c, j].astype(F32)
         for land in (5, 6, 7):
             total = total + tb[land, j].astype(F32)
@@ -680,7 +672,7 @@
     reduce3(3)
     ys[...] = dot(unperm[...], fin[...]).astype(BF16)
 
-    b_left = exchange(ys, back, b_send, b_recv)
+    b_left = exchange(ys, back, b_sems)
     spots = lax.broadcasted_iota(jnp.int32, (T, GRID), 1).astype(F32)
     result = resid
     for i in range(TOPK):
@@ -688,17 +680,18 @@
         result = result + dot(picked, back[...])[:, 0:SHARE] * column(weight_ref[i : i + 1, :])
     out_ref[...] = result.astype(BF16)
 
-    for p, ident, off, flip, to in started:
-        wcopy(p, ident, slot(off, flip), to).wait_send()
-    for g in lats + gathers:
-        g.finish()
-    for i in range(1, NCTX):
-        rcopy((c + i) % NCTX, c).wait_send()
-    for j in range(4):
-        for i in range(10):
-            scopy(j, i).wait_send()
-    a_left()
-    b_left()
+    for p, group in ((0, 0), (3, 1), (5, 2)):
+        wcopy(p, pieces(p, NEXP - 1), w_recv.at[0, 0], sibling).wait_send()
+    seven = pl.ds(0, NCTX - 1)
+    for sent, sem in (
+        (latb.at[seven, pl.ds(0, MASKED)], l_send),
+        (parts.at[seven], r_send),
+        (xa.at[seven], g_send),
+        (pd.at[seven], s_send),
+    ):
+        remote(sent, sent, sem.at[0], r_recv.at[0], ctx=yp).wait_send()
+    a_left.wait_send()
+    b_left.wait_send()
 
 
 def permutations():
@@ -711,7 +704,6 @@
 
 
 VMEM = pl.BlockSpec(memory_space=pltpu.VMEM)
-SMEM = pl.BlockSpec(memory_space=pltpu.SMEM)
 ANY = pl.BlockSpec(memory_space=pl.ANY)
 
 
@@ -735,7 +727,7 @@
     return pl.pallas_call(
         functools.partial(layer_kernel, scale=1.0 / math.sqrt(DN + DR)),
         out_shape=jax.ShapeDtypeStruct((T, SHARE), BF16),
-        in_specs=[ANY] * 6 + [VMEM, SMEM, VMEM, VMEM] + [ANY] * 5,
+        in_specs=[ANY] * 15,
         out_specs=VMEM,
         scratch_shapes=[
             pltpu.VMEM((NEXP, HL, 16, DN), BF16),
@@ -752,6 +744,10 @@
             pltpu.VMEM((NCTX, T, WIDE), BF16),
             pltpu.VMEM((T, HL * (DN + DR)), BF16),
             pltpu.VMEM((SHARE, T), BF16),
+            pltpu.VMEM((D // 128, 128), F32),
+            pltpu.VMEM((32, 32), jnp.int32),
+            pltpu.VMEM((TOPK, T), jnp.int32),
+            pltpu.VMEM((TOPK, T), F32),
             pltpu.VMEM((SLOTS, GRID), BF16),
             pltpu.VMEM((GRID, SLOTS), BF16),
             pltpu.VMEM((4, D, FFL), BF16),
@@ -765,21 +761,20 @@
             pltpu.VMEM((SLOTS, WIDE), BF16),
             pltpu.VMEM((GRID, WIDE), BF16),
             pltpu.VMEM((GRID, WIDE), BF16),
-            dma((11,)),
-            dma((6, 32)),
-            dma((6, 32)),
-            dma((2, 8)),
-            dma((2, 8)),
-            dma((NCTX,)),
-            dma((NCTX,)),
-            dma((NEXP,)),
-            dma((NEXP,)),
-            dma((4, 8)),
-            dma((4, 8)),
-            dma((4, 10)),
-            dma((4, 10)),
-            dma((NEXP,)),
-            dma((NEXP,)),
+            dma((15,)),
+            dma((3,)),
+            dma((5, 8)),
+            dma((10,)),
+            dma((1,)),
+            dma((2, 5)),
+            dma((1,)),
+            dma((1,)),
+            dma((2,)),
+            dma((1,)),
+            dma((4, 5)),
+            dma((1,)),
+            dma((4, 4)),
+            dma((2,)),
         ],
         compiler_params=pltpu.CompilerParams(
             collective_id=0, has_side_effects=True, vmem_limit_bytes=54 * 1024 * 1024

time: 167 us -> 159 us (0.952)
  Pallas kernels: 165 us -> 158 us
    pallas_call x1, Pallas kernels: 165 us -> 158 us  [local(): pl.pallas_call(functools.partial(layer_kernel, scale=1.0 / math.sqrt(DN +...]
where the time goes in v3:
time: 159 us
  Pallas kernels  158 us (99%)
  local copies, waits for them, and re-layouts  1.67 us (1%)
    pallas_call x1, Pallas kernels, local(): pl.pallas_call(functools.partial(layer_kernel, scale=1.0 / math.sqrt(DN +...  158 us

profile of v3, /device:TPU:1, one launch (start us, length us, event | category | flops | bytes accessed | tf_op | source)
XLA Modules:
  0.0 159.2 jit_solution(10000977719971021479)
XLA Ops:
  0.0 157.5 %layer.1 = bf16[128,448]{1,0:T(8,128)(2,1)} custom-call(bf16[128,1536]{1,0:T(8,128)(2,1)} %q_ref.1, bf16[576,512]{1,0:T(8,128)(2,1)} %bitcast.9, bf16[8,16,128]{2,1,0:T(8,128)(2,1)} %bitcast.12, bf16[8,16,128]{2,1,0:T(8,128)(2,1)} %av_ref.1, bf16[112,1024]{1,0:T(8,128)(2,1)} %bitcast.10, bf16[448,128]{1,0:T(8,128)(2,1)} %bitcast.11, f32[28,128]{1,0:T(8,128)} %bitcast.13, ...), custom_call_target="tpu_custom_call" | custom-call | tf_op jit(solution)/shard_map/layer/pallas_call | solution.py:727
  157.5 1.7 %copy.16 = bf16[128,448]{0,1:T(8,128)(2,1)} copy(bf16[128,448]{1,0:T(8,128)(2,1)} %layer.1) | data formatting | bytes 229376 | tf_op jit(solution)/shard_map/layer/pallas_call | solution.py:727

commit v4 on v3

--- a/solution.py
+++ b/solution.py
@@ -19,6 +19,7 @@
 BLK = 128
 SHARE = 448
 WIDE = 512
+MAIN = 384
 T = 128
 NCTX = 8
 NEXP = 32
@@ -240,20 +241,13 @@
 
     barrier = pltpu.get_barrier_semaphore()
 
-    def hello(i, carry):
-        pl.semaphore_signal(
-            barrier, inc=1, device_id={"exp": (e + i) % NEXP}, device_id_type=MESH
-        )
-        return carry
-
-    lax.fori_loop(1, NEXP, hello, 0)
-    for i in range(1, NCTX):
-        pl.semaphore_signal(
-            barrier, inc=1, device_id={"ctx": (c + i) % NCTX}, device_id_type=MESH
-        )
+    peers = [{"exp": d} for d in (up, down, partner, sibling)]
+    peers += [{"ctx": (c + i) % NCTX} for i in range(1, NCTX)]
+    for where in peers:
+        pl.semaphore_signal(barrier, inc=1, device_id=where, device_id_type=MESH)
     for copy in early + [mask_copy]:
         copy.start()
-    pl.semaphore_wait(barrier, NEXP - 1 + NCTX - 1)
+    pl.semaphore_wait(barrier, len(peers))
 
 
     def piece(p, block):
@@ -518,9 +512,22 @@
     gains = jnp.concatenate([gain_ref[pl.ds(x * 7 + i, 1), :] for i in range(7)], axis=1)
     gain = jnp.where(y == 0, gains[:, 0:SHARE], gains[:, SHARE:])
     scaled = jnp.concatenate([resid * gain, tail], axis=1).astype(BF16)
-    where = lax.broadcasted_iota(jnp.int32, (GRID, T), 0).astype(F32)
-    chosen = (where == place_rows[0]) | (where == place_rows[1])
-    xs[...] = dot(jnp.where(chosen, 1.0, 0.0).astype(BF16), scaled).astype(BF16)
+    row = lax.broadcasted_iota(jnp.int32, (GRID, T), 0)
+    where = row.astype(F32)
+    fourth = row % 4 == 3
+
+    def chosen(at):
+        return (at == place_rows[0]) | (at == place_rows[1])
+
+    def pick(mask):
+        return jnp.where(mask, 1.0, 0.0).astype(BF16)
+
+    tails = [
+        dot(pick(chosen(where - (3 - i)) & fourth), scaled[:, MAIN:WIDE]) for i in range(3)
+    ]
+    xs[...] = (
+        dot(pick(chosen(where)), scaled[:, 0:MAIN]) + jnp.concatenate(tails, axis=1)
+    ).astype(BF16)
 
     def rows16(i):
         return pl.ds(pl.multiple_of(i * 16, 16), 16)
@@ -541,7 +548,10 @@
 
     a_left = exchange(xs, rx, a_sems)
     for j in range(4):
-        xa[c, j] = dot(perm[j * ROWS : (j + 1) * ROWS, :], rx[...]).astype(BF16)
+        rows = slice(j * ROWS, (j + 1) * ROWS)
+        xa[c, j, :, 0:MAIN] = dot(perm[0, rows, :], rx[...]).astype(BF16)
+        tail = sum(dot(perm[1 + i, rows, :], rx[:, i * 128 : (i + 1) * 128]) for i in range(3))
+        xa[c, j, :, MAIN:WIDE] = tail.astype(BF16)
 
     def rows_view(j):
         return lambda block, first, rows: xa.at[block, j, pl.ds(first, rows)]
@@ -670,14 +680,25 @@
     reduce2(3)
     reduce3(2)
     reduce3(3)
-    ys[...] = dot(unperm[...], fin[...]).astype(BF16)
+    tails = [dot(unperm[1 + i], fin[:, MAIN:WIDE]) for i in range(3)]
+    ys[...] = (dot(unperm[0], fin[:, 0:MAIN]) + jnp.concatenate(tails, axis=1)).astype(BF16)
 
     b_left = exchange(ys, back, b_sems)
-    spots = lax.broadcasted_iota(jnp.int32, (T, GRID), 1).astype(F32)
+    spot = lax.broadcasted_iota(jnp.int32, (T, GRID), 1)
+    spots = spot.astype(F32)
+    fourth = spot % 4 == 3
     result = resid
     for i in range(TOPK):
-        picked = jnp.where(spots == place_cols[i], 1.0, 0.0).astype(BF16)
-        result = result + dot(picked, back[...])[:, 0:SHARE] * column(weight_ref[i : i + 1, :])
+        main = dot(pick(spots == place_cols[i]), back[...])
+        tail = sum(
+            dot(
+                pick((spots - (3 - n) == place_cols[i]) & fourth),
+                back[:, n * 128 : (n + 1) * 128],
+            )
+            for n in range(3)
+        )
+        both = jnp.concatenate([main, tail[:, 0 : SHARE - MAIN]], axis=1)
+        result = result + both * column(weight_ref[i : i + 1, :])
     out_ref[...] = result.astype(BF16)
 
     for p, group in ((0, 0), (3, 1), (5, 2)):
@@ -695,11 +716,12 @@
 
 
 def permutations():
-    perm = np.zeros((SLOTS, GRID), np.float32)
+    perm = np.zeros((4, SLOTS, GRID), np.float32)
     for j in range(4):
         for s in range(NEXP):
             for i in range(3):
-                perm[j * ROWS + s * 3 + i, s * 16 + j * 4 + i] = 1.0
+                perm[0, j * ROWS + s * 3 + i, s * 16 + j * 4 + i] = 1.0
+                perm[1 + i, j * ROWS + s * 3 + i, s * 16 + j * 4 + 3] = 1.0
     return perm
 
 
@@ -748,19 +770,19 @@
             pltpu.VMEM((32, 32), jnp.int32),
             pltpu.VMEM((TOPK, T), jnp.int32),
             pltpu.VMEM((TOPK, T), F32),
-            pltpu.VMEM((SLOTS, GRID), BF16),
-            pltpu.VMEM((GRID, SLOTS), BF16),
+            pltpu.VMEM((4, SLOTS, GRID), BF16),
+            pltpu.VMEM((4, GRID, SLOTS), BF16),
             pltpu.VMEM((4, D, FFL), BF16),
             pltpu.VMEM((4, D, FFL), BF16),
             pltpu.VMEM((4, FFL, D), BF16),
-            pltpu.VMEM((GRID, WIDE), BF16),
-            pltpu.VMEM((GRID, WIDE), BF16),
+            pltpu.VMEM((GRID, MAIN), BF16),
+            pltpu.VMEM((GRID, MAIN), BF16),
             pltpu.VMEM((NCTX, 4, ROWS, WIDE), BF16),
             pltpu.VMEM((NCTX, 4, ROWS, WIDE), BF16),
             pltpu.VMEM((8, 4, ROWS, WIDE), BF16),
             pltpu.VMEM((SLOTS, WIDE), BF16),
-            pltpu.VMEM((GRID, WIDE), BF16),
-            pltpu.VMEM((GRID, WIDE), BF16),
+            pltpu.VMEM((GRID, MAIN), BF16),
+            pltpu.VMEM((GRID, MAIN), BF16),
             dma((15,)),
             dma((3,)),
             dma((5, 8)),
@@ -777,7 +799,7 @@
             dma((2,)),
         ],
         compiler_params=pltpu.CompilerParams(
-            collective_id=0, has_side_effects=True, vmem_limit_bytes=54 * 1024 * 1024
+            collective_id=0, has_side_effects=True, vmem_limit_bytes=56 * 1024 * 1024
         ),
         name="layer",
     )(
@@ -792,7 +814,7 @@
         routes.T,
         route_weight.T,
         jnp.asarray(perm, BF16),
-        jnp.asarray(perm.T, BF16),
+        jnp.asarray(perm.transpose(0, 2, 1), BF16),
         w_gate,
         w_up,
         w_down,

time: 159 us -> 152 us (0.956)
  Pallas kernels: 158 us -> 150 us
    pallas_call x1, Pallas kernels: 158 us -> 150 us  [local(): pl.pallas_call(functools.partial(layer_kernel, scale=1.0 / math.sqrt(DN +...]
where the time goes in v4:
time: 152 us
  Pallas kernels  150 us (99%)
  local copies, waits for them, and re-layouts  1.67 us (1%)
    pallas_call x1, Pallas kernels, local(): pl.pallas_call(functools.partial(layer_kernel, scale=1.0 / math.sqrt(DN +...  150 us

profile of v4, /device:TPU:1, one launch (start us, length us, event | category | flops | bytes accessed | tf_op | source)
XLA Modules:
  0.0 152.1 jit_solution(12090066288804832835)
XLA Ops:
  0.0 150.4 %layer.1 = bf16[128,448]{1,0:T(8,128)(2,1)} custom-call(bf16[128,1536]{1,0:T(8,128)(2,1)} %q_ref.1, bf16[576,512]{1,0:T(8,128)(2,1)} %bitcast.9, bf16[8,16,128]{2,1,0:T(8,128)(2,1)} %bitcast.12, bf16[8,16,128]{2,1,0:T(8,128)(2,1)} %av_ref.1, bf16[112,1024]{1,0:T(8,128)(2,1)} %bitcast.10, bf16[448,128]{1,0:T(8,128)(2,1)} %bitcast.11, f32[28,128]{1,0:T(8,128)} %bitcast.13, ...), custom_call_target="tpu_custom_call" | custom-call | tf_op jit(solution)/shard_map/layer/pallas_call | solution.py:749
  150.4 1.7 %copy.16 = bf16[128,448]{0,1:T(8,128)(2,1)} copy(bf16[128,448]{1,0:T(8,128)(2,1)} %layer.1) | data formatting | bytes 229376 | tf_op jit(solution)/shard_map/layer/pallas_call | solution.py:749

commit v5 on v4

--- a/solution.py
+++ b/solution.py
@@ -39,24 +39,24 @@
 CAUSAL = MASKED + 16
 DEPTH = CAUSAL + T
 HALF_LAT = (DC + DR) // 2
-PIECE_ROWS = {1: (0, 32), 2: (32, 32), 4: (64, 48), 5: (0, WO)}
+PIECE_ROWS = {1: (0, 48), 2: (48, 32), 4: (80, 32), 5: (0, WO)}
 LAST_PIECE = 4
 
 PLAN = (
-    ("first", 0), ("latents", 0), ("latents", 1), ("first", 1), ("first", 2), ("prepare",), ("ring", 0, 1, 0),
-    ("partner", 0), ("first", 4), ("ring", 0, 2, 0), ("ring", 0, 1, 1), ("ring", 1, 1, 0), ("first", 3),
-    ("halves", 0), ("spread", 0), ("ring", 0, 3, 0), ("ring", 0, 2, 1), ("ring", 2, 1, 0), ("ring", 1, 2, 0),
-    ("ring", 0, 3, 1), ("ring", 3, 1, 0), ("ring", 4, 1, 0), ("halves", 1), ("ring", 2, 2, 0), ("spread", 1),
-    ("ring", 1, 3, 0), ("partner", 1), ("far", 0), ("cross", 0), ("partner", 2), ("absorb",), ("partner", 3),
-    ("partner", 4), ("attend", 0, 0), ("ring", 3, 2, 0), ("attend", 0, 1), ("ring", 1, 1, 1),
-    ("ring", 4, 2, 0), ("attend", 0, 2), ("attend", 0, 3), ("cross", 1), ("ring", 2, 1, 1), ("attend", 1, 0),
-    ("ring", 3, 1, 1), ("ring", 4, 1, 1), ("attend", 1, 1), ("ring", 1, 2, 1), ("attend", 1, 2),
-    ("ring", 2, 3, 0), ("attend", 1, 3), ("ring", 2, 2, 1), ("attend", 2, 0), ("ring", 3, 2, 1),
-    ("ring", 3, 3, 0), ("attend", 2, 1), ("ring", 4, 2, 1), ("attend", 2, 2), ("ring", 4, 3, 0),
-    ("attend", 2, 3), ("attend", 3, 0), ("ring", 1, 3, 1), ("ring", 2, 3, 1), ("ring", 3, 3, 1),
-    ("attend", 3, 1), ("attend", 3, 2), ("ring", 4, 3, 1), ("attend", 3, 3), ("far", 1), ("far", 2),
-    ("far", 3), ("far", 4), ("values",), ("project", 0), ("project", 1), ("project", -1), ("project", 2),
-    ("project", -2), ("project", 3), ("project", -3), ("project", 4),
+    ("first", 0), ("latents", 0), ("latents", 1), ("first", 1), ("prepare",), ("ring", 0, 1, 0),
+    ("partner", 0), ("first", 2), ("ring", 0, 2, 0), ("ring", 0, 1, 1), ("first", 4), ("halves", 0),
+    ("ring", 0, 3, 0), ("spread", 0), ("ring", 0, 2, 1), ("ring", 1, 1, 0), ("ring", 0, 3, 1),
+    ("ring", 2, 1, 0), ("ring", 4, 1, 0), ("first", 3), ("ring", 1, 2, 0), ("halves", 1), ("spread", 1),
+    ("far", 0), ("ring", 2, 2, 0), ("partner", 1), ("cross", 0), ("absorb",), ("ring", 3, 1, 0),
+    ("attend", 0, 0), ("partner", 3), ("partner", 2), ("attend", 0, 1), ("partner", 4), ("attend", 0, 2),
+    ("ring", 1, 1, 1), ("attend", 0, 3), ("ring", 3, 1, 1), ("attend", 1, 0), ("cross", 1), ("ring", 3, 2, 0),
+    ("ring", 2, 1, 1), ("attend", 1, 1), ("ring", 4, 1, 1), ("attend", 1, 2), ("ring", 4, 2, 0),
+    ("ring", 3, 2, 1), ("attend", 1, 3), ("ring", 3, 3, 0), ("ring", 1, 2, 1), ("attend", 2, 0),
+    ("attend", 2, 1), ("ring", 2, 2, 1), ("ring", 4, 2, 1), ("attend", 2, 2), ("ring", 3, 3, 1),
+    ("ring", 1, 3, 0), ("attend", 2, 3), ("attend", 3, 0), ("ring", 2, 3, 0), ("attend", 3, 1),
+    ("ring", 4, 3, 0), ("far", 3), ("ring", 1, 3, 1), ("ring", 2, 3, 1), ("ring", 4, 3, 1), ("attend", 3, 2),
+    ("attend", 3, 3), ("values",), ("far", 1), ("far", 2), ("project", 0), ("project", 1), ("far", 4),
+    ("project", -1), ("project", 2), ("project", -2), ("project", 3), ("project", -3), ("project", 4),
 )
 
 

time: 152 us -> 149 us (0.980)
  Pallas kernels: 150 us -> 147 us
    pallas_call x1, Pallas kernels: 150 us -> 147 us  [local(): pl.pallas_call(functools.partial(layer_kernel, scale=1.0 / math.sqrt(DN +...]
where the time goes in v5:
time: 149 us
  Pallas kernels  147 us (99%)
  local copies, waits for them, and re-layouts  1.67 us (1%)
    pallas_call x1, Pallas kernels, local(): pl.pallas_call(functools.partial(layer_kernel, scale=1.0 / math.sqrt(DN +...  147 us

profile of v5, /device:TPU:1, one launch (start us, length us, event | category | flops | bytes accessed | tf_op | source)
XLA Modules:
  0.0 148.7 jit_solution(17671181530903687972)
XLA Ops:
  0.0 147.1 %layer.1 = bf16[128,448]{1,0:T(8,128)(2,1)} custom-call(bf16[128,1536]{1,0:T(8,128)(2,1)} %q_ref.1, bf16[576,512]{1,0:T(8,128)(2,1)} %bitcast.9, bf16[8,16,128]{2,1,0:T(8,128)(2,1)} %bitcast.12, bf16[8,16,128]{2,1,0:T(8,128)(2,1)} %av_ref.1, bf16[112,1024]{1,0:T(8,128)(2,1)} %bitcast.10, bf16[448,128]{1,0:T(8,128)(2,1)} %bitcast.11, f32[28,128]{1,0:T(8,128)} %bitcast.13, ...), custom_call_target="tpu_custom_call" | custom-call | tf_op jit(solution)/shard_map/layer/pallas_call | solution.py:749
  147.1 1.7 %copy.16 = bf16[128,448]{0,1:T(8,128)(2,1)} copy(bf16[128,448]{1,0:T(8,128)(2,1)} %layer.1) | data formatting | bytes 229376 | tf_op jit(solution)/shard_map/layer/pallas_call | solution.py:749
